TPU v7x, 32 devices: a whole 2x2x4 slice. The times are simulated.
32 devices in a mesh: section: 2 (over core), dp: 16 (over z, y, x).
Axes of the slice: x: 2, y: 2, z: 4, core: 2. Of those that a mesh axis runs over, the one named last changes fastest.
Arguments:
- reduce_weight: bfloat16 [2048, 512], P('dp'), may hold values from -0.125 to 0.125
- dilated_weight: bfloat16 [4608, 512], P('dp'), may hold values from -0.09375 to 0.09375
- expand_weight: bfloat16 [512, 2048], P('dp'), may hold values from -0.25 to 0.25
- reduce_gain: float32 [512], replicated, may hold values from 0.5 to 1.5
- reduce_bias: float32 [512], replicated, may hold values from -1.5 to 1.5
- dilated_gain: float32 [512], replicated, may hold values from 0.5 to 1.5
- dilated_bias: float32 [512], replicated, may hold values from -1.5 to 1.5
- expand_gain: float32 [2048], replicated, may hold values from 0.5 to 1.5
- expand_bias: float32 [2048], replicated, may hold values from -1.5 to 1.5
- head_conv: bfloat16 [18432, 768], P('dp'), may hold values from -0.046875 to 0.046875
- head_gain: float32 [768], replicated, may hold values from 0.5 to 1.5
- head_bias: float32 [768], replicated, may hold values from -1.5 to 1.5
- seg_proj: bfloat16 [256, 13], replicated, may hold values from -0.75 to 0.75
- depth_proj: bfloat16 [256, 1], replicated, may hold values from -1.5 to 1.5
- normal_proj: bfloat16 [256, 3], replicated, may hold values from -0.75 to 0.75
- small_feats: bfloat16 [1536, 2048], P('dp'), may hold values from -6 to 6
- small_labels: int32 [1536], P('dp'), may hold values from -1 to 12
- small_depth: float32 [1536], P('dp'), may hold values from 0.5 to 10
- small_normals: float32 [3, 1536], P(None, 'dp'), may hold values from -3 to 3
- small_depth_valid: int32 [1536], P('dp'), may hold values 0 or 1
- small_normal_valid: int32 [1536], P('dp'), may hold values 0 or 1
- large_feats: bfloat16 [2560, 2048], P('dp'), may hold values from -6 to 6
- large_labels: int32 [2560], P('dp'), may hold values from -1 to 12
- large_depth: float32 [2560], P('dp'), may hold values from 0.5 to 10
- large_normals: float32 [3, 2560], P(None, 'dp'), may hold values from -3 to 3
- large_depth_valid: int32 [2560], P('dp'), may hold values 0 or 1
- large_normal_valid: int32 [2560], P('dp'), may hold values 0 or 1
Outputs:
- small_out: bfloat16 [1536, 2048], P('dp')
- large_out: bfloat16 [2560, 2048], P('dp')
- small_input_grad: float32 [1536, 2048], P('dp', 'section')
- large_input_grad: float32 [2560, 2048], P('dp', 'section')
- reduce_weight_grad: float32 [2048, 512], P('dp')
- dilated_weight_grad: float32 [4608, 512], P('dp')
- expand_weight_grad: float32 [512, 2048], P('dp')
- reduce_gain_grad: float32 [512], replicated
- reduce_bias_grad: float32 [512], replicated
- dilated_gain_grad: float32 [512], replicated
- dilated_bias_grad: float32 [512], replicated
- expand_gain_grad: float32 [2048], replicated
- expand_bias_grad: float32 [2048], replicated
- head_conv_grad: float32 [18432, 768], P('dp')
- head_gain_grad: float32 [768], replicated
- head_bias_grad: float32 [768], replicated
- seg_proj_grad: float32 [256, 13], replicated
- depth_proj_grad: float32 [256, 1], replicated
- normal_proj_grad: float32 [256, 3], replicated
All inputs are finite; a program needn't handle non-finite values. No bound on the sum of `small_depth_valid` or of `small_normal_valid` or of `large_depth_valid` or of `large_normal_valid` on one device may be relied on, other than what follows from the above.
Results may differ from a plain program's by a relative error of at most 0.02.
Values may be sent and summed in bfloat16 or wider, within the bound.
A program may use at most 320 MiB of HBM per device.

v0:
```python
import jax
import jax.numpy as jnp
from jax import lax
from jax.sharding import PartitionSpec as P

C = 2048
BOT = 512
HEADW = 256
NCLS = 13
WS = 48
WL = 80
HS = 36
HL = 60


EPS = 1e-05
RIDGE = 0.1
SWEEPS = 5
HIGH = lax.Precision.HIGHEST
CONTRACT_ROWS = (((0,), (0,)), ((), ()))
CONTRACT_COLS = (((1,), (1,)), ((), ()))


def extended_2(value, sides, width):
    for axis, dim in sides:
        devices, length = (lax.axis_size(axis), value.shape[dim])
        up = [(i, (i + 1) % devices) for i in range(devices - 1)]
        down = [(j, i) for i, j in up]
        last = lax.slice_in_dim(value, length - width, length, axis=dim)
        first = lax.slice_in_dim(value, 0, width, axis=dim)
        before = lax.ppermute(last, axis, up)
        after = lax.ppermute(first, axis, down)
        value = jnp.concatenate([before, value, after], axis=dim)
    return value


def shifted(block, axis, distance):
    devices = range(lax.axis_size(axis))
    route = [(i - distance, i) for i in devices if i - distance in devices]
    return lax.ppermute(block, axis, route)


def silu_slope(value):
    sigma = jax.nn.sigmoid(value)
    return sigma * (1.0 + value * (1.0 - sigma))


def small_product(left, right):
    return jnp.sum(left[:, :, None] * right[None, :, :], axis=1)


def row_masks(row_count, strip, height, start):
    local = start + jnp.arange(row_count, dtype=jnp.int32)
    stacked = []
    for tap_row in range(3):
        other = local + 2 * (tap_row - 1)
        keep = (other >= 0) & (other < strip) & (other // height == local // height)
        stacked.append(keep.astype(jnp.float32))
    return jnp.stack(stacked)


def align_weights(gram):
    identity = jnp.eye(3, dtype=jnp.float32)
    matrix = gram + RIDGE * jnp.trace(gram) / 3.0 * identity
    vectors = identity
    for sweep in range(SWEEPS):
        for first_i, second_i in ((0, 1), (0, 2), (1, 2)):
            angle = 0.5 * jnp.arctan2(
                2.0 * matrix[first_i, second_i],
                matrix[second_i, second_i] - matrix[first_i, first_i],
            )
            cosine = jnp.cos(angle)
            sine = jnp.sin(angle)
            rotate = identity.at[first_i, first_i].set(cosine).at[second_i, second_i].set(cosine)
            rotate = rotate.at[first_i, second_i].set(sine).at[second_i, first_i].set(-sine)
            matrix = small_product(rotate.T, small_product(matrix, rotate))
            vectors = small_product(vectors, rotate)
    values = jnp.diagonal(matrix)
    inverse_root = small_product(vectors * lax.rsqrt(values)[None, :], vectors.T)
    return jnp.sqrt(jnp.min(values)) * jnp.sum(inverse_root, axis=1)


def forward_patches(extended, masks, width):
    row_count = extended.shape[0] - 4
    padded = jnp.pad(extended, ((0, 0), (2, 2), (0, 0)))
    pieces = []
    for tap_row in range(3):
        row_keep = masks[tap_row][:, None, None].astype(extended.dtype)
        for tap_col in range(3):
            piece = padded[
                2 * tap_row : 2 * tap_row + row_count, 2 * tap_col : 2 * tap_col + width, :
            ]
            pieces.append(piece * row_keep)
    return jnp.concatenate(pieces, axis=2).reshape(row_count * width, -1)


def backward_patches(extended, masks, width):
    row_count = extended.shape[0] - 4
    padded = jnp.pad(extended, ((0, 0), (2, 2), (0, 0)))
    pieces = []
    for tap_row in range(3):
        row_start = 2 * (2 - tap_row)
        row_keep = masks[2 - tap_row][:, None, None].astype(extended.dtype)
        for tap_col in range(3):
            col_start = 2 * (2 - tap_col)
            piece = padded[row_start : row_start + row_count, col_start : col_start + width, :]
            pieces.append(piece * row_keep)
    return jnp.concatenate(pieces, axis=2).reshape(row_count * width, -1)


def block_moments(values):
    return lax.psum((values[0], values[1]), "dp")


def head_moments(values):
    return lax.psum(values, "dp")


def block_rim(grid):
    return extended_2(grid, (("dp", 0),), 2)


def send_up(value):
    return shifted(value, "section", 1)


def send_down(value):
    return shifted(value, "section", -1)


def block_reduce(grads):
    return (
        lax.psum_scatter(grads[0], "dp", scatter_dimension=0, tiled=True),
        lax.psum_scatter(grads[1], "dp", scatter_dimension=0, tiled=True),
        lax.psum_scatter(grads[2], "dp", scatter_dimension=0, tiled=True),
    )


def head_reduce(grad):
    return lax.psum_scatter(grad, "dp", scatter_dimension=0, tiled=True)


def norm_forward(pre, count):
    sums = block_moments((jnp.sum(pre, axis=0), jnp.sum(pre * pre, axis=0)))
    mean = sums[0] / count
    inv_std = lax.rsqrt(sums[1] / count - mean * mean + EPS)
    return ((pre - mean) * inv_std, inv_std)


def norm_backward(grad_out, hat, inv_std, gain, count):
    sums = block_moments((jnp.sum(grad_out, axis=0), jnp.sum(grad_out * hat, axis=0)))
    grad_pre = gain * inv_std * (grad_out - sums[0] / count - hat * (sums[1] / count))
    return (grad_pre, sums[1], sums[0])


def add_tuples(first, second):
    return tuple((earlier + extra for earlier, extra in zip(first, second)))


def block_forward(feats, block_weights, block_norms, info):
    width, masks, count = info
    reduce_w, dilated_w, expand_w = block_weights
    reduce_gain, reduce_bias, dilated_gain, dilated_bias, expand_gain, expand_bias = block_norms
    row_count = feats.shape[0] // width
    pre_one = jnp.dot(feats, reduce_w, preferred_element_type=jnp.float32)
    hat_one, inv_one = norm_forward(pre_one, count)
    act_one = jax.nn.silu(hat_one * reduce_gain + reduce_bias).astype(jnp.bfloat16)
    extended = block_rim(act_one.reshape(row_count, width, BOT))
    patches = forward_patches(extended, masks, width)
    pre_two = jnp.dot(patches, dilated_w, preferred_element_type=jnp.float32)
    hat_two, inv_two = norm_forward(pre_two, count)
    act_two = jax.nn.silu(hat_two * dilated_gain + dilated_bias).astype(jnp.bfloat16)
    pre_three = jnp.dot(act_two, expand_w, preferred_element_type=jnp.float32)
    hat_three, inv_three = norm_forward(pre_three, count)
    output = jax.nn.silu(hat_three * expand_gain + expand_bias + feats.astype(jnp.float32)).astype(
        jnp.bfloat16
    )
    return (output, (patches, act_two, hat_one, hat_two, hat_three, inv_one, inv_two, inv_three))


def block_backward(arriving, feats, kept, block_weights, block_norms, info, sums):
    width, masks, count = info
    patches, act_two, hat_one, hat_two, hat_three, inv_one, inv_two, inv_three = kept
    reduce_w, dilated_w, expand_w = block_weights
    reduce_gain, reduce_bias, dilated_gain, dilated_bias, expand_gain, expand_bias = block_norms
    row_count = feats.shape[0] // width
    residual = hat_three * expand_gain + expand_bias + feats.astype(jnp.float32)
    grad_sum = arriving.astype(jnp.float32) * silu_slope(residual)
    grad_three, gain_three, bias_three = norm_backward(
        grad_sum, hat_three, inv_three, expand_gain, count
    )
    grad_three = grad_three.astype(jnp.bfloat16)
    expand_grad = lax.dot_general(
        act_two, grad_three, CONTRACT_ROWS, preferred_element_type=jnp.float32
    )
    back_two = lax.dot_general(
        grad_three, expand_w, CONTRACT_COLS, preferred_element_type=jnp.float32
    )
    back_two = back_two * silu_slope(hat_two * dilated_gain + dilated_bias)
    grad_two, gain_two, bias_two = norm_backward(back_two, hat_two, inv_two, dilated_gain, count)
    grad_two = grad_two.astype(jnp.bfloat16)
    dilated_grad = lax.dot_general(
        patches, grad_two, CONTRACT_ROWS, preferred_element_type=jnp.float32
    )
    extended = block_rim(grad_two.reshape(row_count, width, BOT))
    back_taps = backward_patches(extended, masks, width).reshape(-1, 9, BOT)
    back_one = jnp.einsum(
        "pkc,kic->pi", back_taps, dilated_w.reshape(9, BOT, BOT), preferred_element_type=jnp.float32
    )
    back_one = back_one * silu_slope(hat_one * reduce_gain + reduce_bias)
    grad_one, gain_one, bias_one = norm_backward(back_one, hat_one, inv_one, reduce_gain, count)
    grad_one = grad_one.astype(jnp.bfloat16)
    reduce_grad = lax.dot_general(
        feats, grad_one, CONTRACT_ROWS, preferred_element_type=jnp.float32
    )
    input_grad = grad_sum + lax.dot_general(
        grad_one, reduce_w, CONTRACT_COLS, preferred_element_type=jnp.float32
    )
    weight_grads = (reduce_grad, dilated_grad, expand_grad)
    moved = block_reduce(weight_grads)
    norm_grads = (gain_one, bias_one, gain_two, bias_two, gain_three, bias_three)
    return (input_grad, (add_tuples(sums[0], moved), add_tuples(sums[1], norm_grads)))


def head_step(arriving, kernel, head_params, targets, info, sums):
    head_gain, head_bias, seg_proj, depth_proj, normal_proj = head_params
    labels, depth, normals, depth_valid, normal_valid = targets
    width, masks, count = info
    row_count = arriving.shape[0] // width
    extended = extended_2(arriving.reshape(row_count, width, C), (("dp", 0),), 2)
    patches = forward_patches(extended, masks, width)
    pre = jnp.dot(patches, kernel, preferred_element_type=jnp.float32)
    seg_valid = (labels >= 0).astype(jnp.float32)
    depth_keep = depth_valid.astype(jnp.float32)
    normal_keep = normal_valid.astype(jnp.float32)
    local_counts = jnp.stack([jnp.sum(seg_valid), jnp.sum(depth_keep), jnp.sum(normal_keep)])
    moments = head_moments((jnp.sum(pre, axis=0), jnp.sum(pre * pre, axis=0), local_counts))
    mean = moments[0] / count
    inv_std = lax.rsqrt(moments[1] / count - mean * mean + EPS)
    hat = (pre - mean) * inv_std
    counts = jnp.maximum(moments[2], 1.0)
    normed = hat * head_gain + head_bias
    act = jax.nn.silu(normed).astype(jnp.bfloat16)
    seg_act = act[:, :HEADW]
    depth_act = act[:, HEADW : 2 * HEADW]
    normal_act = act[:, 2 * HEADW :]
    logits = jnp.dot(seg_act, seg_proj, preferred_element_type=jnp.float32)
    depth_pred = jnp.dot(depth_act, depth_proj, preferred_element_type=jnp.float32)[:, 0]
    normal_pred = jnp.dot(normal_act, normal_proj, preferred_element_type=jnp.float32)
    onehot = (labels[:, None] == jnp.arange(NCLS, dtype=jnp.int32)[None, :]).astype(jnp.float32)
    grad_logits = (jax.nn.softmax(logits, axis=1) - onehot) * (seg_valid / counts[0])[:, None]
    gap = depth_pred - depth
    grad_depth = (depth_keep / counts[1] * gap * lax.rsqrt(gap * gap + 1.0))[:, None]
    target = normals.T
    radius = jnp.sqrt(jnp.sum(normal_pred * normal_pred, axis=1) + 1.0)
    along = jnp.sum(normal_pred * target, axis=1)
    grad_normal = -(normal_keep / counts[2])[:, None] * (
        target / radius[:, None] - (along / radius**3)[:, None] * normal_pred
    )
    seg_grad = lax.dot_general(
        seg_act.astype(jnp.float32), grad_logits, CONTRACT_ROWS, precision=HIGH
    )
    depth_grad = lax.dot_general(
        depth_act.astype(jnp.float32), grad_depth, CONTRACT_ROWS, precision=HIGH
    )
    normal_grad = lax.dot_general(
        normal_act.astype(jnp.float32), grad_normal, CONTRACT_ROWS, precision=HIGH
    )
    grad_act = jnp.concatenate(
        [
            lax.dot_general(
                grad_logits, seg_proj.astype(jnp.float32), CONTRACT_COLS, precision=HIGH
            ),
            lax.dot_general(
                grad_depth, depth_proj.astype(jnp.float32), CONTRACT_COLS, precision=HIGH
            ),
            lax.dot_general(
                grad_normal, normal_proj.astype(jnp.float32), CONTRACT_COLS, precision=HIGH
            ),
        ],
        axis=1,
    )
    grad_normed = grad_act * silu_slope(normed)
    totals = head_moments(
        (
            jnp.sum(grad_normed, axis=0),
            jnp.sum(grad_normed * hat, axis=0),
            seg_grad,
            depth_grad,
            normal_grad,
        )
    )
    grad_pre = (
        head_gain * inv_std * (grad_normed - totals[0] / count - hat * (totals[1] / count))
    ).astype(jnp.bfloat16)
    kernel_grad = lax.dot_general(
        patches, grad_pre, CONTRACT_ROWS, preferred_element_type=jnp.float32
    )
    back = extended_2(grad_pre.reshape(row_count, width, 3 * HEADW), (("dp", 0),), 2)
    back_taps = backward_patches(back, masks, width).reshape(-1, 9, 3, HEADW)
    task_grads = jnp.einsum(
        "pktc,kitc->tpi",
        back_taps,
        kernel.reshape(9, C, 3, HEADW),
        preferred_element_type=jnp.float32,
    )
    local_gram = jnp.einsum("tpi,spi->ts", task_grads, task_grads, precision=HIGH)
    gram = lax.psum(local_gram, "dp")
    alpha = align_weights(gram)
    down = jnp.einsum("t,tpi->pi", alpha, task_grads, precision=HIGH).astype(jnp.bfloat16)
    moved = head_reduce(kernel_grad)
    small_grads = (totals[1], totals[0], totals[2], totals[3], totals[4])
    return (down, (sums[0] + moved, add_tuples(sums[1], small_grads)))


def body(
    reduce_weight,
    dilated_weight,
    expand_weight,
    reduce_gain,
    reduce_bias,
    dilated_gain,
    dilated_bias,
    expand_gain,
    expand_bias,
    head_conv,
    head_gain,
    head_bias,
    seg_proj,
    depth_proj,
    normal_proj,
    small_feats,
    small_labels,
    small_depth,
    small_normals,
    small_depth_valid,
    small_normal_valid,
    large_feats,
    large_labels,
    large_depth,
    large_normals,
    large_depth_valid,
    large_normal_valid,
):
    leading = lax.axis_index("section") == 0
    small_feats = jnp.where(leading, small_feats, jnp.zeros_like(small_feats))
    large_feats = jnp.where(leading, large_feats, jnp.zeros_like(large_feats))
    dp_count = lax.axis_size("dp")
    dp_index = lax.axis_index("dp")
    row_count = small_feats.shape[0] // WS
    strip = row_count * dp_count
    small_info = (
        WS,
        row_masks(row_count, strip, HS, dp_index * row_count),
        row_count * WS * dp_count,
    )
    large_info = (
        WL,
        row_masks(row_count, strip, HL, dp_index * row_count),
        row_count * WL * dp_count,
    )
    block_norms = (reduce_gain, reduce_bias, dilated_gain, dilated_bias, expand_gain, expand_bias)
    head_params = (head_gain, head_bias, seg_proj, depth_proj, normal_proj)
    small_targets = (
        small_labels,
        small_depth,
        small_normals,
        small_depth_valid,
        small_normal_valid,
    )
    large_targets = (
        large_labels,
        large_depth,
        large_normals,
        large_depth_valid,
        large_normal_valid,
    )
    block_sums = (
        (
            jnp.zeros((C // dp_count, BOT), jnp.float32),
            jnp.zeros((9 * BOT // dp_count, BOT), jnp.float32),
            jnp.zeros((BOT // dp_count, C), jnp.float32),
        ),
        (
            jnp.zeros((BOT,), jnp.float32),
            jnp.zeros((BOT,), jnp.float32),
            jnp.zeros((BOT,), jnp.float32),
            jnp.zeros((BOT,), jnp.float32),
            jnp.zeros((C,), jnp.float32),
            jnp.zeros((C,), jnp.float32),
        ),
    )
    head_sums = (
        jnp.zeros((9 * C // dp_count, 3 * HEADW), jnp.float32),
        (
            jnp.zeros((3 * HEADW,), jnp.float32),
            jnp.zeros((3 * HEADW,), jnp.float32),
            jnp.zeros((HEADW, NCLS), jnp.float32),
            jnp.zeros((HEADW, 1), jnp.float32),
            jnp.zeros((HEADW, 3), jnp.float32),
        ),
    )
    block_weights = (
        lax.all_gather(reduce_weight, "dp", axis=0, tiled=True),
        lax.all_gather(dilated_weight, "dp", axis=0, tiled=True),
        lax.all_gather(expand_weight, "dp", axis=0, tiled=True),
    )
    kernel = lax.all_gather(head_conv, "dp", axis=0, tiled=True)
    small_out, small_kept = block_forward(small_feats, block_weights, block_norms, small_info)
    small_in = send_up(small_out)
    large_out, large_kept = block_forward(large_feats, block_weights, block_norms, large_info)
    small_down, head_sums = head_step(
        small_in, kernel, head_params, small_targets, small_info, head_sums
    )
    large_in = send_up(large_out)
    small_back = send_down(small_down)
    small_grad, block_sums = block_backward(
        small_back, small_feats, small_kept, block_weights, block_norms, small_info, block_sums
    )
    large_down, head_sums = head_step(
        large_in, kernel, head_params, large_targets, large_info, head_sums
    )
    large_back = send_down(large_down)
    large_grad, block_sums = block_backward(
        large_back, large_feats, large_kept, block_weights, block_norms, large_info, block_sums
    )
    block_shards, kernel_shard = (block_sums[0], head_sums[0])
    half = C // lax.axis_size("section")
    norm_grads = block_sums[1]
    lifted = (
        shifted(block_shards[0].astype(jnp.bfloat16), "section", 1).astype(jnp.float32),
        shifted(block_shards[1].astype(jnp.bfloat16), "section", 1).astype(jnp.float32),
        shifted(block_shards[2].astype(jnp.bfloat16), "section", 1).astype(jnp.float32),
        shifted(norm_grads[0].astype(jnp.bfloat16), "section", 1).astype(jnp.float32),
        shifted(norm_grads[1].astype(jnp.bfloat16), "section", 1).astype(jnp.float32),
        shifted(norm_grads[2].astype(jnp.bfloat16), "section", 1).astype(jnp.float32),
        shifted(norm_grads[3].astype(jnp.bfloat16), "section", 1).astype(jnp.float32),
        shifted(norm_grads[4].astype(jnp.bfloat16), "section", 1).astype(jnp.float32),
        shifted(norm_grads[5].astype(jnp.bfloat16), "section", 1).astype(jnp.float32),
        shifted(small_grad[:, half:].astype(jnp.bfloat16), "section", 1).astype(jnp.float32),
        shifted(large_grad[:, half:].astype(jnp.bfloat16), "section", 1).astype(jnp.float32),
    )
    head_small = head_sums[1]
    lowered = (
        shifted(kernel_shard.astype(jnp.bfloat16), "section", -1).astype(kernel_shard.dtype),
        shifted(head_small[0].astype(jnp.bfloat16), "section", -1).astype(jnp.float32),
        shifted(head_small[1].astype(jnp.bfloat16), "section", -1).astype(jnp.float32),
        shifted(head_small[2].astype(jnp.bfloat16), "section", -1).astype(jnp.float32),
        shifted(head_small[3].astype(jnp.bfloat16), "section", -1).astype(jnp.float32),
        shifted(head_small[4].astype(jnp.bfloat16), "section", -1).astype(jnp.float32),
    )

    def pick(lead_value, tail_value):
        return jnp.where(leading, lead_value, tail_value)

    return (
        pick(small_out, small_in),
        pick(large_out, large_in),
        pick(small_grad[:, :half], lifted[9]),
        pick(large_grad[:, :half], lifted[10]),
        pick(block_shards[0], lifted[0]),
        pick(block_shards[1], lifted[1]),
        pick(block_shards[2], lifted[2]),
        pick(norm_grads[0], lifted[3]),
        pick(norm_grads[1], lifted[4]),
        pick(norm_grads[2], lifted[5]),
        pick(norm_grads[3], lifted[6]),
        pick(norm_grads[4], lifted[7]),
        pick(norm_grads[5], lifted[8]),
        pick(lowered[0], kernel_shard),
        pick(lowered[1], head_small[0]),
        pick(lowered[2], head_small[1]),
        pick(lowered[3], head_small[2]),
        pick(lowered[4], head_small[3]),
        pick(lowered[5], head_small[4]),
    )


def solution(mesh):
    in_specs = (
        P("dp", None),
        P("dp", None),
        P("dp", None),
        P(),
        P(),
        P(),
        P(),
        P(),
        P(),
        P("dp", None),
        P(),
        P(),
        P(),
        P(),
        P(),
        P("dp", None),
        P("dp"),
        P("dp"),
        P(None, "dp"),
        P("dp"),
        P("dp"),
        P("dp", None),
        P("dp"),
        P("dp"),
        P(None, "dp"),
        P("dp"),
        P("dp"),
    )
    out_specs = (
        P("dp", None),
        P("dp", None),
        P("dp", "section"),
        P("dp", "section"),
        P("dp", None),
        P("dp", None),
        P("dp", None),
        P(),
        P(),
        P(),
        P(),
        P(),
        P(),
        P("dp", None),
        P(),
        P(),
        P(),
        P(),
        P(),
    )
    return jax.shard_map(body, mesh=mesh, in_specs=in_specs, out_specs=out_specs, check_vma=False)
```

profile of v0, /device:TPU:1, one launch (start us, length us, event | category | flops | bytes accessed | tf_op | source)
XLA Modules:
  0.0 2005.5 jit_solution(14824164263725703742)
XLA Ops:
  11.4 61.8 %all-gather.5.cloned.1.call-done = bf16[2048,512]{1,0:T(8,128)(2,1)} async-done(((bf16[128,512]{1,0:T(8,128)(2,1)}), bf16[2048,512]{1,0:T(8,128)(2,1)}) %all-gather.5.cloned.1.call-update) | async-done | bytes 2097168 | tf_op jit(solution)/shard_map/all_gather | solution.py:404
  76.0 33.0 %all-reduce.16 = (f32[512]{0:T(512)S(1)}, f32[512]{0:T(512)S(1)}, f32[512]{0:T(512)S(1)}, f32[512]{0:T(512)S(1)}) all-reduce(f32[512]{0:T(512)S(1)} %get-tuple-element.1490, f32[512]{0:T(512)S(1)} %get-tuple-element.1489, f32[512]{0:T(512)S(1)} %get-tuple-element.1478, ...), channel_id=1, replica_groups=mesh['section'=2,'dp'=16] {'dp'}, use_global_device_ids=true, to_apply=%region_3.4 | all-reduce | flops 2048 | bytes 16384 | tf_op jit(solution)/shard_map/psum | solution.py:112
  125.0 34.2 %all-gather.7.cloned.1.call-done = bf16[4608,512]{1,0:T(8,128)(2,1)} async-done(((bf16[288,512]{1,0:T(8,128)(2,1)}), bf16[4608,512]{1,0:T(8,128)(2,1)}) %all-gather.7.cloned.1.call-update) | async-done | bytes 4718608 | tf_op jit(solution)/shard_map/all_gather | solution.py:405
  164.5 33.9 %all-reduce.15 = (f32[512]{0:T(512)S(1)}, f32[512]{0:T(512)S(1)}, f32[512]{0:T(512)S(1)}, f32[512]{0:T(512)S(1)}) all-reduce(f32[512]{0:T(512)S(1)} %get-tuple-element.1488, f32[512]{0:T(512)S(1)} %get-tuple-element.1487, f32[512]{0:T(512)S(1)} %get-tuple-element.1476, ...), channel_id=1, replica_groups=mesh['section'=2,'dp'=16] {'dp'}, use_global_device_ids=true, to_apply=%region_7.8 | all-reduce | flops 2048 | bytes 16384 | tf_op jit(solution)/shard_map/psum | solution.py:112
  199.0 23.4 %all-gather.9.cloned.1.call-done = bf16[512,2048]{1,0:T(8,128)(2,1)} async-done(((bf16[32,2048]{1,0:T(8,128)(2,1)}), bf16[512,2048]{1,0:T(8,128)(2,1)}) %all-gather.9.cloned.1.call-update) | async-done | bytes 2097168 | tf_op jit(solution)/shard_map/all_gather | solution.py:406
  225.5 62.1 %all-reduce.14 = (f32[2048]{0:T(1024)S(1)}, f32[2048]{0:T(1024)S(1)}, f32[2048]{0:T(1024)S(1)}, f32[2048]{0:T(1024)S(1)}) all-reduce(f32[2048]{0:T(1024)S(1)} %get-tuple-element.1466, f32[2048]{0:T(1024)S(1)} %get-tuple-element.1465, f32[2048]{0:T(1024)S(1)} %get-tuple-element.1462, ...), channel_id=1, replica_groups=mesh['section'=2,'dp'=16] {'dp'}, use_global_device_ids=true, to_apply=%region_11.12 | all-reduce | flops 8192 | bytes 65536 | tf_op jit(solution)/shard_map/psum | solution.py:112
  293.1 13.4 collective-permute-done.2
  330.4 10.8 collective-permute-done.7
  343.0 32.1 %collective-permute-done.14 = bf16[2,80,2048]{2,1,0:T(8,128)(2,1)S(1)} collective-permute-done((bf16[2,80,2048]{2,1,0:T(8,128)(2,1)S(1)}, bf16[2,80,2048]{2,1,0:T(8,128)(2,1)S(1)}, u32[]{:S(2)}, u32[]{:S(2)}) %collective-permute-start.14) | collective-permute-done | bytes 655392 | tf_op jit(solution)/shard_map/ppermute | solution.py:31
  390.0 181.0 %all-gather.11.cloned.1.call-done = bf16[18432,768]{1,0:T(8,128)(2,1)} async-done(((bf16[1152,768]{1,0:T(8,128)(2,1)}), bf16[18432,768]{1,0:T(8,128)(2,1)}) %all-gather.11.cloned.1.call-update) | async-done | bytes 28311568 | tf_op jit(solution)/shard_map/all_gather | solution.py:408
  571.0 16.9 fusion.180
  587.9 12.9 fusion.186
  600.8 60.6 %all-reduce.13 = (f32[768]{0:T(1024)}, f32[768]{0:T(1024)}, f32[3]{0:T(128)}, f32[768]{0:T(1024)}, f32[768]{0:T(1024)}, /*index=5*/f32[3]{0:T(128)}) all-reduce(f32[768]{0:T(1024)} %get-tuple-element.1482, f32[768]{0:T(1024)} %get-tuple-element.1481, f32[3]{0:T(128)} %get-tuple-element.1792, ...), channel_id=1, replica_groups=mesh['section'=2,'dp'=16] {'dp'}, use_global_device_ids=true, to_apply=%region_25.26 | all-reduce | flops 3078 | bytes 24624 | tf_op jit(solution)/shard_map/psum | solution.py:116
  687.7 58.3 %all-reduce.12 = (f32[768]{0:T(1024)S(1)}, f32[768]{0:T(1024)}, f32[768]{0:T(1024)}, f32[768]{0:T(1024)}) all-reduce(f32[768]{0:T(1024)} %get-tuple-element.1480, f32[768]{0:T(1024)} %get-tuple-element.1479, f32[768]{0:T(1024)S(1)} %get-tuple-element.1468, f32[768]{0:T(1024)S(1)} %get-tuple-element.1467), channel_id=1, replica_groups=mesh['section'=2,'dp'=16] {'dp'}, use_global_device_ids=true, to_apply=%region_39.40 | all-reduce | flops 3072 | bytes 24576 | tf_op jit(solution)/shard_map/psum | solution.py:116
  749.9 23.4 %fusion.238 = f32[18432,768]{1,0:T(8,128)} fusion(bf16[160,18432]{1,0:T(8,128)(2,1)} %bitcast.47, bf16[160,768]{1,0:T(8,128)(2,1)S(1)} %multiply_convert_fusion.4), kind=kOutput, calls=%fused_computation.613 | convolution fusion | flops 4529848320 | bytes 62767104 | tf_op jit(solution)/shard_map/dot_general | solution.py:296
  774.2 36.4 %convolution_add_fusion = f32[18432,768]{1,0:T(8,128)} fusion(f32[18432,768]{1,0:T(8,128)} %fusion.238, bf16[96,18432]{1,0:T(8,128)(2,1)S(1)} %bitcast.173, bf16[96,768]{1,0:T(8,128)(2,1)} %multiply_convert_fusion.10), kind=kOutput, calls=%fused_computation.2 | convolution fusion | flops 2732064768 | bytes 116932608 | tf_op jit(solution)/shard_map/dot_general | solution.py:296
  827.4 61.8 %reshape.3565 = bf16[9,2048,3,256]{3,2,1,0:T(4,128)(2,1)} reshape(bf16[18432,768]{1,0:T(8,128)(2,1)} %all-gather.11.cloned.1.call-done) | data formatting | bytes 56623104 | tf_op jit(solution)/shard_map/reshape | solution.py:304
  894.5 21.0 %fusion.16 = f32[3,96,2048]{2,1,0:T(8,128)S(1)} fusion(bf16[9,2048,3,256]{3,2,1,0:T(4,128)(2,1)} %reshape.3565, bf16[96,9,3,256]{3,2,1,0:T(4,128)(2,1)} %reshape_reshape.12), kind=kOutput, calls=%fused_computation.25 | convolution fusion | flops 2717908992 | bytes 31997952 | tf_op jit(solution)/shard_map/pktc,kitc->tpi/dot_general | solution.py:301
  915.6 14.6 fusion.42
  946.4 23.4 %fusion.9 = f32[3,160,2048]{2,1,0:T(8,128)S(1)} fusion(bf16[9,2048,3,256]{3,2,1,0:T(4,128)(2,1)} %reshape.3565, bf16[160,9,3,256]{3,2,1,0:T(4,128)(2,1)} %reshape_reshape.14), kind=kOutput, calls=%fused_computation.20 | convolution fusion | flops 4529848320 | bytes 34455552 | tf_op jit(solution)/shard_map/pktc,kitc->tpi/dot_general | solution.py:301
  970.1 23.5 %fusion.45 = f32[3,3]{1,0:T(4,128)S(1)} fusion(f32[3,160,2048]{2,1,0:T(8,128)S(1)} %fusion.9), kind=kOutput, calls=%fused_computation.68 | convolution fusion | flops 35389440 | bytes 3932196 | tf_op jit(solution)/shard_map/tpi,spi->ts/dot_general | solution.py:307
  994.2 34.2 %all-reduce.11 = (f32[3,3]{1,0:T(4,128)S(1)}, f32[3,3]{1,0:T(4,128)S(1)}) all-reduce(f32[3,3]{1,0:T(4,128)S(1)} %fusion.45, f32[3,3]{1,0:T(4,128)S(1)} %copy-done.154), channel_id=1, replica_groups=mesh['section'=2,'dp'=16] {'dp'}, use_global_device_ids=true, to_apply=%region_119.120 | all-reduce | flops 18 | bytes 144 | tf_op jit(solution)/shard_map/psum | solution.py:308
  1226.2 14.9 fusion.4
  1242.3 39.8 %collective-permute-start.18 = (bf16[160,2048]{1,0:T(8,128)(2,1)}, bf16[160,2048]{1,0:T(8,128)(2,1)}, u32[]{:S(2)}, u32[]{:S(2)}) collective-permute-start(bf16[160,2048]{1,0:T(8,128)(2,1)} %bitcast.170), channel_id=1, source_target_pairs={{16,0},{17,1},{18,2},{19,3},{20,4},{21,5},{22,6},{23,7},{24,8},{25... | collective-permute-start | bytes 1966088 | tf_op jit(solution)/shard_map/ppermute | solution.py:40
  1297.6 61.9 %all-reduce.10 = (f32[2048]{0:T(1024)S(1)}, f32[2048]{0:T(1024)S(1)}, f32[2048]{0:T(1024)S(1)}, f32[2048]{0:T(1024)}) all-reduce(f32[2048]{0:T(1024)S(1)} %get-tuple-element.1464, f32[2048]{0:T(1024)S(1)} %get-tuple-element.1463, f32[2048]{0:T(1024)S(1)} %get-tuple-element.1460, ...), channel_id=1, replica_groups=mesh['section'=2,'dp'=16] {'dp'}, use_global_device_ids=true, to_apply=%region_94.95 | all-reduce | flops 8192 | bytes 65536 | tf_op jit(solution)/shard_map/psum | solution.py:112
  1374.5 32.7 %all-reduce.9 = (f32[512]{0:T(512)S(1)}, f32[512]{0:T(512)S(1)}, f32[512]{0:T(512)S(1)}, f32[512]{0:T(512)S(1)}) all-reduce(f32[512]{0:T(512)S(1)} %get-tuple-element.1486, f32[512]{0:T(512)S(1)} %get-tuple-element.1485, f32[512]{0:T(512)S(1)} %get-tuple-element.1474, ...), channel_id=1, replica_groups=mesh['section'=2,'dp'=16] {'dp'}, use_global_device_ids=true, to_apply=%region_98.99 | all-reduce | flops 2048 | bytes 16384 | tf_op jit(solution)/shard_map/psum | solution.py:112
  1452.4 61.2 %all-reduce.8 = (f32[512]{0:T(512)S(1)}, f32[512]{0:T(512)S(1)}, f32[512]{0:T(512)S(1)}, f32[512]{0:T(512)S(1)}, f32[256,13]{0,1:T(8,128)S(1)}, /*index=5*/f32[256,1]{0,1:T(1,128)}, f32[256,3]{0,1:T(4,128)S(1)}) all-reduce(f32[512]{0:T(512)S(1)} %get-tuple-element.1484, ...), channel_id=1, replica_groups=mesh['section'=2,'dp'=16] {'dp'}, use_global_device_ids=true, to_apply=%region_102.103 | all-reduce | flops 6400 | bytes 51200 | tf_op jit(solution)/shard_map/psum | solution.py:112
  1530.7 40.9 %collective-permute-start.33 = (bf16[768]{0:T(1024)(128)(2,1)S(1)}, bf16[768]{0:T(1024)(128)(2,1)S(1)}, u32[]{:S(2)}, u32[]{:S(2)}) collective-permute-start(bf16[768]{0:T(1024)(128)(2,1)S(1)} %copy-done.196), channel_id=1, source_target_pairs={{16,0},{17,1},{18,2},{19,3},{20,4},{21,5},{22,6},{23,7},{24,8},{25... | collective-permute-start | bytes 4616 | tf_op jit(solution)/shard_map/ppermute | solution.py:40
  1598.9 20.3 %reduce-scatter.11.cloned.1.call-done = f32[1152,768]{1,0:T(8,128)} async-done(((f32[18432,768]{1,0:T(8,128)}), f32[1152,768]{1,0:T(8,128)}) %reduce-scatter.11.cloned.1.call-update) | async-done | bytes 3538960 | tf_op jit(solution)/shard_map/reduce_scatter | solution.py:140
  1629.0 85.8 %reduce-scatter.9.cloned.1.call-done = f32[32,2048]{1,0:T(8,128)} async-done(((f32[512,2048]{1,0:T(8,128)}), f32[32,2048]{1,0:T(8,128)}) %reduce-scatter.9.cloned.1.call-update) | async-done | bytes 262160 | tf_op jit(solution)/shard_map/reduce_scatter | solution.py:135
  1718.6 93.2 %reduce-scatter.5.cloned.1.call-done = f32[128,512]{1,0:T(8,128)} async-done(((f32[2048,512]{1,0:T(8,128)}), f32[128,512]{1,0:T(8,128)}) %reduce-scatter.5.cloned.1.call-update) | async-done | bytes 262160 | tf_op jit(solution)/shard_map/reduce_scatter | solution.py:133
  1814.7 173.0 %reduce-scatter.7.cloned.1.call-done = f32[288,512]{1,0:T(8,128)} async-done(((f32[4608,512]{1,0:T(8,128)}), f32[288,512]{1,0:T(8,128)}) %reduce-scatter.7.cloned.1.call-update) | async-done | bytes 589840 | tf_op jit(solution)/shard_map/reduce_scatter | solution.py:134
  (1015 shorter events, 395.2 us)
Async XLA Ops:
  7.2 66.0 %all-gather.5.cloned.1.call-start = ((), (), s32[]{:S(2)}) async-start(), calls=%async_computation.4 | async-start | bytes 2228224 | tf_op jit(solution)/shard_map/all_gather | solution.py:404
  8.0 151.2 %all-gather.7.cloned.1.call-start = ((), (), s32[]{:S(2)}) async-start(), calls=%async_computation.5 | async-start | bytes 5013504 | tf_op jit(solution)/shard_map/all_gather | solution.py:405
  8.7 213.7 %all-gather.9.cloned.1.call-start = ((), (), s32[]{:S(2)}) async-start(), calls=%async_computation.6 | async-start | bytes 2228224 | tf_op jit(solution)/shard_map/all_gather | solution.py:406
  9.5 561.5 %all-gather.11.cloned.1.call-start = ((), (), s32[]{:S(2)}) async-start(), calls=%async_computation.7 | async-start | bytes 30081024 | tf_op jit(solution)/shard_map/all_gather | solution.py:408
  10.0 1609.1 %reduce-scatter.11.cloned.1.call-start = ((), (), s32[]{:S(2)}) async-start(), calls=%async_computation.11 | async-start | bytes 60162048 | tf_op jit(solution)/shard_map/reduce_scatter | solution.py:140
  109.8 8.3 collective-permute-start
  288.7 17.9 collective-permute-start.2
  290.6 24.9 %collective-permute-start.5 = (bf16[160,2048]{1,0:T(8,128)(2,1)S(1)}, bf16[160,2048]{1,0:T(8,128)(2,1)S(1)}, u32[]{:S(2)}, u32[]{:S(2)}) collective-permute-start(bf16[160,2048]{1,0:T(8,128)(2,1)S(1)} %multiply_convert_fusion.1), channel_id=1, source_target_pairs={{0,16},{1,17},{2,18},{3,19},{4,20},{5,21},{6,22},{7,23},{8,24},{9,... | collective-permute-start | bytes 1966088 | tf_op jit(solution)/shard_map/ppermute | solution.py:40
  306.6 23.8 %collective-permute-start.6 = (bf16[2,48,2048]{2,1,0:T(8,128)(2,1)S(1)}, bf16[2,48,2048]{2,1,0:T(8,128)(2,1)S(1)}, u32[]{:S(2)}, u32[]{:S(2)}) collective-permute-start(bf16[2,48,2048]{2,1,0:T(8,128)(2,1)S(1)} %bitcast.188), channel_id=1, source_target_pairs={{0,1},{1,2},{2,3},{3,4},{4,5},{5,6},{6,7},{7,8},{8,9},{9,10},{10,1... | collective-permute-start | bytes 1179656 | tf_op jit(solution)/shard_map/ppermute | solution.py:31
  307.9 33.4 %collective-permute-start.7 = (bf16[2,48,2048]{2,1,0:T(8,128)(2,1)S(1)}, bf16[2,48,2048]{2,1,0:T(8,128)(2,1)S(1)}, u32[]{:S(2)}, u32[]{:S(2)}) collective-permute-start(bf16[2,48,2048]{2,1,0:T(8,128)(2,1)S(1)} %bitcast.189), channel_id=1, source_target_pairs={{1,0},{2,1},{3,2},{4,3},{5,4},{6,5},{7,6},{8,7},{9,8},{10,9},{11,1... | collective-permute-start | bytes 1179656 | tf_op jit(solution)/shard_map/ppermute | solution.py:32
  315.5 59.6 %collective-permute-start.14 = (bf16[2,80,2048]{2,1,0:T(8,128)(2,1)S(1)}, bf16[2,80,2048]{2,1,0:T(8,128)(2,1)S(1)}, u32[]{:S(2)}, u32[]{:S(2)}) collective-permute-start(bf16[2,80,2048]{2,1,0:T(8,128)(2,1)S(1)} %bitcast.178), channel_id=1, source_target_pairs={{0,1},{1,2},{2,3},{3,4},{4,5},{5,6},{6,7},{7,8},{8,9},{9,10},{10,1... | collective-permute-start | bytes 1966088 | tf_op jit(solution)/shard_map/ppermute | solution.py:31
  319.5 60.2 %collective-permute-start.15 = (bf16[2,80,2048]{2,1,0:T(8,128)(2,1)S(1)}, bf16[2,80,2048]{2,1,0:T(8,128)(2,1)S(1)}, u32[]{:S(2)}, u32[]{:S(2)}) collective-permute-start(bf16[2,80,2048]{2,1,0:T(8,128)(2,1)S(1)} %bitcast.179), channel_id=1, source_target_pairs={{1,0},{2,1},{3,2},{4,3},{5,4},{6,5},{7,6},{8,7},{9,8},{10,9},{11,1... | collective-permute-start | bytes 1966088 | tf_op jit(solution)/shard_map/ppermute | solution.py:32
  810.6 904.2 %reduce-scatter.9.cloned.1.call-start = ((), (), s32[]{:S(2)}) async-start(), calls=%async_computation.10 | async-start | bytes 4456448 | tf_op jit(solution)/shard_map/reduce_scatter | solution.py:135
  819.2 111.1 %collective-permute-start.16 = (bf16[2,80,768]{2,1,0:T(8,128)(2,1)S(1)}, bf16[2,80,768]{2,1,0:T(8,128)(2,1)S(1)}, u32[]{:S(2)}, u32[]{:S(2)}) collective-permute-start(bf16[2,80,768]{2,1,0:T(8,128)(2,1)S(1)} %bitcast.184), channel_id=1, source_target_pairs={{0,1},{1,2},{2,3},{3,4},{4,5},{5,6},{6,7},{7,8},{8,9},{9,10},{10,1... | collective-permute-start | bytes 737288 | tf_op jit(solution)/shard_map/ppermute | solution.py:31
  820.5 109.8 %collective-permute-start.17 = (bf16[2,80,768]{2,1,0:T(8,128)(2,1)S(1)}, bf16[2,80,768]{2,1,0:T(8,128)(2,1)}, u32[]{:S(2)}, u32[]{:S(2)}) collective-permute-start(bf16[2,80,768]{2,1,0:T(8,128)(2,1)S(1)} %bitcast.185), channel_id=1, source_target_pairs={{1,0},{2,1},{3,2},{4,3},{5,4},{6,5},{7,6},{8,7},{9,8},{10,9},{11,1... | collective-permute-start | bytes 737288 | tf_op jit(solution)/shard_map/ppermute | solution.py:32
  821.9 69.6 %collective-permute-start.8 = (bf16[2,48,768]{2,1,0:T(8,128)(2,1)S(1)}, bf16[2,48,768]{2,1,0:T(8,128)(2,1)S(1)}, u32[]{:S(2)}, u32[]{:S(2)}) collective-permute-start(bf16[2,48,768]{2,1,0:T(8,128)(2,1)S(1)} %bitcast.196), channel_id=1, source_target_pairs={{0,1},{1,2},{2,3},{3,4},{4,5},{5,6},{6,7},{7,8},{8,9},{9,10},{10,1... | collective-permute-start | bytes 442376 | tf_op jit(solution)/shard_map/ppermute | solution.py:31
  826.1 65.5 %collective-permute-start.9 = (bf16[2,48,768]{2,1,0:T(8,128)(2,1)S(1)}, bf16[2,48,768]{2,1,0:T(8,128)(2,1)S(1)}, u32[]{:S(2)}, u32[]{:S(2)}) collective-permute-start(bf16[2,48,768]{2,1,0:T(8,128)(2,1)S(1)} %bitcast.197), channel_id=1, source_target_pairs={{1,0},{2,1},{3,2},{4,3},{5,4},{6,5},{7,6},{8,7},{9,8},{10,9},{11,1... | collective-permute-start | bytes 442376 | tf_op jit(solution)/shard_map/ppermute | solution.py:32
  1242.3 53.3 %collective-permute-start.18 = (bf16[160,2048]{1,0:T(8,128)(2,1)}, bf16[160,2048]{1,0:T(8,128)(2,1)}, u32[]{:S(2)}, u32[]{:S(2)}) collective-permute-start(bf16[160,2048]{1,0:T(8,128)(2,1)} %bitcast.170), channel_id=1, source_target_pairs={{16,0},{17,1},{18,2},{19,3},{20,4},{21,5},{22,6},{23,7},{24,8},{25... | collective-permute-start | bytes 1966088 | tf_op jit(solution)/shard_map/ppermute | solution.py:40
  1368.5 443.3 %reduce-scatter.5.cloned.1.call-start = ((), (), s32[]{:S(2)}) async-start(), calls=%async_computation.8 | async-start | bytes 4456448 | tf_op jit(solution)/shard_map/reduce_scatter | solution.py:133
  1409.4 11.4 collective-permute-start.11
  1412.8 8.0 collective-permute-start.12
  1415.2 20.0 collective-permute-start.19
  1419.3 16.0 collective-permute-start.20
  1520.7 467.0 %reduce-scatter.7.cloned.1.call-start = ((), (), s32[]{:S(2)}) async-start(), calls=%async_computation.9 | async-start | bytes 10027008 | tf_op jit(solution)/shard_map/reduce_scatter | solution.py:134
  1530.7 44.2 %collective-permute-start.33 = (bf16[768]{0:T(1024)(128)(2,1)S(1)}, bf16[768]{0:T(1024)(128)(2,1)S(1)}, u32[]{:S(2)}, u32[]{:S(2)}) collective-permute-start(bf16[768]{0:T(1024)(128)(2,1)S(1)} %copy-done.196), channel_id=1, source_target_pairs={{16,0},{17,1},{18,2},{19,3},{20,4},{21,5},{22,6},{23,7},{24,8},{25... | collective-permute-start | bytes 4616 | tf_op jit(solution)/shard_map/ppermute | solution.py:40
  1584.9 41.4 %collective-permute-start.36 = (bf16[256,3]{0,1:T(4,128)(2,1)S(1)}, bf16[256,3]{0,1:T(4,128)(2,1)}, u32[]{:S(2)}, u32[]{:S(2)}) collective-permute-start(bf16[256,3]{0,1:T(4,128)(2,1)S(1)} %convert_element_type.455), channel_id=1, source_target_pairs={{16,0},{17,1},{18,2},{19,3},{20,4},{21,5},{22,6},{23,7},{24,8},{25... | collective-permute-start | bytes 4616 | tf_op jit(solution)/shard_map/ppermute | solution.py:40
  1588.9 38.7 %collective-permute-start.34 = (bf16[256,13]{0,1:T(8,128)(2,1)S(1)}, bf16[256,13]{0,1:T(8,128)(2,1)S(1)}, u32[]{:S(2)}, u32[]{:S(2)}) collective-permute-start(bf16[256,13]{0,1:T(8,128)(2,1)S(1)} %convert_element_type.451), channel_id=1, source_target_pairs={{16,0},{17,1},{18,2},{19,3},{20,4},{21,5},{22,6},{23,7},{24,8},{25... | collective-permute-start | bytes 19976 | tf_op jit(solution)/shard_map/ppermute | solution.py:40
  1594.5 123.2 %collective-permute-start.21 = (bf16[160,1024]{1,0:T(8,128)(2,1)S(1)}, bf16[160,1024]{1,0:T(8,128)(2,1)S(1)}, u32[]{:S(2)}, u32[]{:S(2)}) collective-permute-start(bf16[160,1024]{1,0:T(8,128)(2,1)S(1)} %slice.2917), channel_id=1, source_target_pairs={{0,16},{1,17},{2,18},{3,19},{4,20},{5,21},{6,22},{7,23},{8,24},{9,... | collective-permute-start | bytes 983048 | tf_op jit(solution)/shard_map/ppermute | solution.py:40
  1596.4 31.8 %collective-permute-start.13 = (bf16[96,1024]{1,0:T(8,128)(2,1)S(1)}, bf16[96,1024]{1,0:T(8,128)(2,1)S(1)}, u32[]{:S(2)}, u32[]{:S(2)}) collective-permute-start(bf16[96,1024]{1,0:T(8,128)(2,1)S(1)} %slice.2918), channel_id=1, source_target_pairs={{0,16},{1,17},{2,18},{3,19},{4,20},{5,21},{6,22},{7,23},{8,24},{9,... | collective-permute-start | bytes 589832 | tf_op jit(solution)/shard_map/ppermute | solution.py:40
  1622.6 371.8 %collective-permute-start.31 = (bf16[1152,768]{1,0:T(8,128)(2,1)}, bf16[1152,768]{1,0:T(8,128)(2,1)}, u32[]{:S(2)}, u32[]{:S(2)}) collective-permute-start(bf16[1152,768]{1,0:T(8,128)(2,1)} %convert_element_type.445), channel_id=1, source_target_pairs={{16,0},{17,1},{18,2},{19,3},{20,4},{21,5},{22,6},{23,7},{24,8},{25... | collective-permute-start | bytes 5308424 | tf_op jit(solution)/shard_map/ppermute | solution.py:40
  1716.4 273.7 %collective-permute-start.24 = (bf16[32,2048]{1,0:T(8,128)(2,1)}, bf16[32,2048]{1,0:T(8,128)(2,1)}, u32[]{:S(2)}, u32[]{:S(2)}) collective-permute-start(bf16[32,2048]{1,0:T(8,128)(2,1)} %convert_element_type.431), channel_id=1, source_target_pairs={{0,16},{1,17},{2,18},{3,19},{4,20},{5,21},{6,22},{7,23},{8,24},{9,... | collective-permute-start | bytes 393224 | tf_op jit(solution)/shard_map/ppermute | solution.py:40
  1813.4 178.4 %collective-permute-start.22 = (bf16[128,512]{1,0:T(8,128)(2,1)}, bf16[128,512]{1,0:T(8,128)(2,1)}, u32[]{:S(2)}, u32[]{:S(2)}) collective-permute-start(bf16[128,512]{1,0:T(8,128)(2,1)} %convert_element_type.427), channel_id=1, source_target_pairs={{0,16},{1,17},{2,18},{3,19},{4,20},{5,21},{6,22},{7,23},{8,24},{9,... | collective-permute-start | bytes 393224 | tf_op jit(solution)/shard_map/ppermute | solution.py:40
  (227 other events, 10302.9 us)
Sparse Core Ops, SparseCore 0:
  10.8 62.3 all-gather.4
  76.0 83.1 all-gather.6
  162.0 60.4 all-gather.8
  225.1 345.8 all-gather.10
  810.7 808.4 reduce-scatter.10
  1621.3 93.4 reduce-scatter.8
  1717.1 94.6 reduce-scatter.4
  1817.5 170.2 reduce-scatter.6
where the time goes:
time: 2020 us; the launch traced here: 2010 us
  waiting for transfers between devices  751 us (37%)
  blocking collectives  438 us (22%)
  matrix products  249 us (12%)
  local copies, waits for them, and re-layouts  190 us (9%)
  starting transfers between devices  145 us (7%)
  other arithmetic  118 us (6%)
  between operations  114 us (6%)
    psum x6, blocking collectives, block_moments(): return lax.psum((values[0], values[1]), 'dp')  285 us
    all_gather x1, waiting for transfers between devices, body(): kernel = lax.all_gather(head_conv, 'dp', axis=0, tiled=True)  181 us
    reduce_scatter x1, waiting for transfers between devices, block_reduce(): lax.psum_scatter(grads[1], 'dp', scatter_dimension=0, tiled=True)  173 us
    psum x2, blocking collectives, head_moments(): return lax.psum(values, 'dp')  119 us
    ppermute x21, starting transfers between devices, shifted(): return lax.ppermute(block, axis, route)  110 us
    reduce_scatter x1, waiting for transfers between devices, block_reduce(): lax.psum_scatter(grads[0], 'dp', scatter_dimension=0, tiled=True)  93.2 us
    reduce_scatter x1, waiting for transfers between devices, block_reduce(): lax.psum_scatter(grads[2], 'dp', scatter_dimension=0, tiled=True)  85.8 us
    all_gather x1, waiting for transfers between devices, body(): lax.all_gather(reduce_weight, 'dp', axis=0, tiled=True)  61.8 us
  transfers between devices with their start and end apart: 45, of which 15 were waited for; matrix products, arithmetic and copies ran while one was open for 21% of the time, Pallas kernels for 0%

commit v1 on v0

v1 whole, which is shorter than its diff:
```python
import functools

import jax
import jax.numpy as jnp
from jax import lax
from jax.experimental import pallas as pl
from jax.experimental.pallas import tpu as pltpu
from jax.sharding import PartitionSpec as P

C = 2048
BOT = 512
HEADW = 256
NCLS = 13
WS = 48
WL = 80
HS = 36
HL = 60

EPS = 1e-05
RIDGE = 0.1
SWEEPS = 5

F32 = jnp.float32
BF16 = jnp.bfloat16
MESH = pl.DeviceIdType.MESH

LINE = WS + WL
SEGMENTS = ((0, WS), (WS, WL))
HEIGHTS = (HS, HL)
PIX = 2 * LINE
TEAM = 8
CH = C // TEAM
HALF = BOT // 2
WIDE = C // 2
HEADS = 3 * HEADW
TAPS = 9
PROJ = 32
DEPTH_ROW = 16
NORMAL_ROW = 24

NN = (((1,), (0,)), ((), ()))
NT = (((1,), (1,)), ((), ()))
TN = (((0,), (0,)), ((), ()))


def mm(left, right, dims=NN):
    return lax.dot_general(left, right, dims, preferred_element_type=F32)


def flip(rank, bits):
    out = rank
    for bit in (1, 2, 4):
        if bits & bit:
            out = out + bit * (1 - 2 * ((rank // bit) % 2))
    return out


def sigmoid(value):
    return 1.0 / (1.0 + jnp.exp(-value))


def silu(value):
    return value * sigmoid(value)


def slope(value):
    sigma = sigmoid(value)
    return sigma * (1.0 + value * (1.0 - sigma))


def seg_rows(lines):
    for line in range(lines):
        for group, (start, length) in enumerate(SEGMENTS):
            yield group, slice(line * LINE + start, line * LINE + start + length)


def position(rows):
    return lax.broadcasted_iota(jnp.int32, (rows, 1), 0) % LINE


def column_mask(rows, tap_col):
    place = position(rows)
    small = place < WS
    column = jnp.where(small, place, place - WS) + (2 * tap_col - 2)
    width = jnp.where(small, WS, WL)
    return ((column >= 0) & (column < width)).astype(F32)


def sideways(value, tap_col):
    rows = value.shape[0]
    if tap_col == 1:
        return value
    return pltpu.roll(value, (2 - 2 * tap_col) % rows, 0) * column_mask(rows, tap_col)


def jacobi_weights(gram):
    third = (gram[0, 0] + gram[1, 1] + gram[2, 2]) / 3.0 * RIDGE
    matrix = {(i, j): gram[min(i, j), max(i, j)] + (third if i == j else 0.0) for i in range(3) for j in range(3)}
    one, zero = jnp.ones_like(third), jnp.zeros_like(third)
    vectors = {(i, j): one if i == j else zero for i in range(3) for j in range(3)}
    for _ in range(SWEEPS):
        for p, q in ((0, 1), (0, 2), (1, 2)):
            up = 2.0 * matrix[p, q]
            across = matrix[q, q] - matrix[p, p]
            scale = jnp.maximum(jnp.abs(up), jnp.abs(across))
            still = scale == 0.0
            scale = jnp.where(still, 1.0, scale)
            up, across = up / scale, across / scale
            length = jnp.where(still, 1.0, jnp.sqrt(up * up + across * across))
            larger = jnp.sqrt(0.5 + 0.5 * jnp.abs(across) / length)
            smaller = 0.5 * up / (length * larger)
            sign = jnp.where(up < 0.0, -1.0, 1.0)
            cosine = jnp.where(still, 1.0, jnp.where(across >= 0.0, larger, jnp.abs(smaller)))
            sine = jnp.where(still, 0.0, jnp.where(across >= 0.0, smaller, sign * larger))
            for i in range(3):
                first, second = matrix[i, p], matrix[i, q]
                matrix[i, p] = first * cosine - second * sine
                matrix[i, q] = first * sine + second * cosine
                first, second = vectors[i, p], vectors[i, q]
                vectors[i, p] = first * cosine - second * sine
                vectors[i, q] = first * sine + second * cosine
            for j in range(3):
                first, second = matrix[p, j], matrix[q, j]
                matrix[p, j] = first * cosine - second * sine
                matrix[q, j] = first * sine + second * cosine
    values = [matrix[i, i] for i in range(3)]
    least = jnp.sqrt(jnp.minimum(jnp.minimum(values[0], values[1]), values[2]))
    alphas = []
    roots = [lax.rsqrt(value) for value in values]
    sums = [vectors[0, k] + vectors[1, k] + vectors[2, k] for k in range(3)]
    for t in range(3):
        alphas.append(least * sum(vectors[t, k] * roots[k] * sums[k] for k in range(3)))
    return alphas


class Links:
    def __init__(self, send, recv, partner):
        self.send, self.recv, self.partner = send, recv, partner
        self.used_send = self.used_recv = 0
        self.open = []

    def slots(self, count=1):
        first = self.used_recv
        self.used_recv += count
        assert self.used_recv <= self.recv.shape[0]
        return first

    def outs(self, count=1):
        first = self.used_send
        self.used_send += count
        assert self.used_send <= self.send.shape[0]
        return first

    def copy(self, src, dst, device, out, slot):
        return pltpu.make_async_remote_copy(
            src_ref=src, dst_ref=dst, send_sem=self.send.at[out], recv_sem=self.recv.at[slot],
            device_id=device, device_id_type=MESH,
        )

    def put(self, src, dst, device, slot, when=None):
        out = self.outs()
        if when is not None:
            device = tuple(jnp.where(when, to, near) for to, near in zip(device, self.partner))
        make = functools.partial(self.copy, src, dst, device, out, slot)
        if when is None:
            make().start()
            done = lambda: make().wait_send()
        else:
            pl.when(when)(lambda: make().start())
            done = lambda: pl.when(when)(lambda: make().wait_send())
        self.open.append(done)
        return done

    def put_or_keep(self, src, dst, device, slot, mine, when=True):
        pl.when(when & mine)(lambda: pltpu.make_async_copy(src, dst, self.recv.at[slot]).start())
        return self.put(src, dst, device, slot, when & jnp.logical_not(mine))

    def landed(self, dst, slot, when=None):
        wait = lambda: pltpu.make_async_copy(dst, dst, self.recv.at[slot]).wait()
        if when is None:
            wait()
        else:
            pl.when(when)(wait)

    def close(self):
        for done in self.open:
            done()
        self.open = []


def pieces(ref, start, count):
    rows = ref.shape[2]
    at = start
    while at < start + count:
        shard, first = at // rows, at % rows
        length = min(rows - first, start + count - at)
        yield (shard // 4, shard % 4, slice(first, first + length)), slice(at - start, at - start + length)
        at += length


def take_rows(ref, start, count):
    if len(ref.shape) == 2:
        return ref[start:start + count, :]
    found = [ref[(*place, slice(None))] for place, _ in pieces(ref, start, count)]
    return found[0] if len(found) == 1 else jnp.concatenate(found, axis=0)


def put_rows(ref, start, value):
    if len(ref.shape) == 2:
        ref[start:start + value.shape[0], :] = value
        return
    for place, rows in pieces(ref, start, value.shape[0]):
        ref[(*place, slice(None))] = value[rows, :]


def several(count, body):
    if count <= 4:
        for index in range(count):
            body(index)
    else:
        lax.fori_loop(0, count, lambda index, carry: (body(index), carry)[1], 0)


class Shapes:
    def __init__(self, dp):
        self.dp = dp
        self.planes = dp // 4
        self.teams = dp // TEAM
        self.unit = C // dp
        self.units_half = dp // (2 * TEAM)
        self.rows = (C // dp, TAPS * BOT // dp, BOT // dp)
        self.wide = (HALF, HALF, WIDE)
        self.full = (C, TAPS * BOT, BOT)
        self.inside = all(rows % 32 == 0 for rows in self.rows)
        self.borders = 2 * dp > min(HEIGHTS)


def scratch_of(shape):
    planes = shape.planes
    table = {
        "x": ((PIX, C), BF16),
        "xh": ((PIX, WIDE), BF16),
        "wback": ((planes // 2, 4, C // shape.dp, HALF) if shape.inside else (WIDE, HALF), BF16),
        "kernel": ((TAPS, 2, CH // 2, HEADS), BF16),
        "pre1": ((PIX, HALF), F32),
        "pre2": ((PIX, HALF), F32),
        "pre3": ((PIX, WIDE), F32),
        "act1": ((3, 2, PIX, HALF), BF16),
        "act1s": ((3, 3, 2, PIX, HALF), BF16),
        "patch2": ((PIX, TAPS * BOT), BF16),
        "act2": ((2, PIX, HALF), BF16),
        "outb": ((4, 2, PIX, CH // 2), BF16),
        "outs": ((3, 6, 2, PIX, CH // 2), BF16),
        "patch": ((PIX, TAPS * CH), BF16),
        "part": ((8, LINE, HEADS), BF16),
        "partm": ((8, 8, HEADS), F32),
        "parts": ((TEAM, LINE, HEADS), BF16),
        "partsm": ((TEAM, 8, HEADS), F32),
        "preh": ((LINE, HEADS), F32),
        "acth": ((LINE, HEADS), BF16),
        "dyh": ((LINE, HEADS), F32),
        "dph": ((LINE, HEADS), BF16),
        "dpx": ((6, 2, LINE, HEADS), BF16),
        "dps": ((3, 6, PIX, HEADW), BF16),
        "grads": ((3, 4, PIX, CH), F32),
        "doutb": ((4, PIX, CH), BF16),
        "dout": ((4, PIX, CH), BF16),
        "du": ((PIX, WIDE), F32),
        "dpre3": ((PIX, WIDE), BF16),
        "half2": ((2, PIX, HALF), F32),
        "half2r": ((PIX, HALF), F32),
        "dy2": ((PIX, HALF), F32),
        "dp2": ((3, PIX, HALF), BF16),
        "half1": ((2, PIX, HALF), F32),
        "half1r": ((PIX, HALF), F32),
        "dy1": ((PIX, HALF), F32),
        "dp1": ((2, PIX, HALF), BF16),
        "dks": ((TAPS, CH // 2, HEADS), BF16),
        "dkr": ((TAPS, CH // 2, HEADS), BF16),
        "dku": ((TAPS, CH // 2, HEADS), BF16),
        "dproj": ((PROJ, HEADW), F32),
        "head_norm": ((8, HEADS), F32),
        "marks": ((8, LINE), jnp.int32),
        "values": ((16, LINE), F32),
        "proj": ((PROJ, HEADS), BF16),
        "dkg": ((shape.teams, TAPS, shape.unit, HEADS), BF16),
    }
    for name, count, width in (
        ("s1", 4, HALF), ("s2", 4, HALF), ("s3", 4, WIDE), ("t3", 4, WIDE), ("t2", 4, HALF), ("t1", 4, HALF),
        ("sh", 8, HEADS), ("th", 8, HEADS),
    ):
        table[name + "a"] = ((count, 8, width), F32)
        table[name + "b"] = ((planes, 8, width), F32)
    table["gma"] = ((8, 16 + PROJ, HEADW), F32)
    table["gmb"] = ((planes, 16 + PROJ, HEADW), F32)
    for index in range(3):
        rows, wide = shape.rows[index], shape.wide[index]
        if shape.inside:
            table[f"w{index}"] = ((planes, 4, rows, wide), BF16)
            table[f"dw{index}"] = ((planes, 4, rows, wide), BF16)
            table[f"ra{index}"] = ((2, planes, 2, rows // 2, wide), BF16)
            table[f"rb{index}"] = ((2, planes, rows // 2, wide), BF16)
            table[f"rc{index}"] = ((planes, rows, wide), BF16)
    return table


def fused(shape, names, used, *refs):
    env = dict(zip(names, refs))
    r_ = lambda name: env[name]
    s = lax.axis_index("section")
    d = lax.axis_index("dp")
    dp, planes, teams = shape.dp, shape.planes, shape.teams
    other = 1 - s
    plane, spot = d // 4, d % 4
    team, rank = d // TEAM, d % TEAM
    partner = (other, d)
    links = Links(r_("send"), r_("recv"), partner)

    gate = pltpu.get_barrier_semaphore()
    total = 2 * dp
    me = s * dp + d

    def greet(offset, carry):
        to = (me + offset) % total
        pl.semaphore_signal(gate, inc=1, device_id=(to // dp, to % dp), device_id_type=MESH)
        return carry

    lax.fori_loop(1, total, greet, 0)

    x = r_("x")
    for line in range(2):
        x[line * LINE:line * LINE + WS, :] = r_("small_feats")[line * WS:(line + 1) * WS, :]
        x[line * LINE + WS:(line + 1) * LINE, :] = r_("large_feats")[line * WL:(line + 1) * WL, :]
    marks, values, proj = r_("marks"), r_("values"), r_("proj")
    head_norm = r_("head_norm")
    for row, name in enumerate(("head_gain", "head_bias")):
        for part in range(HEADS // 128):
            head_norm[row:row + 1, part * 128:(part + 1) * 128] = r_(name)[part:part + 1, :]

    def own_line(section):
        small, large = slice(section * WS, (section + 1) * WS), slice(section * WL, (section + 1) * WL)
        for row, name in enumerate(("labels", "depth_valid", "normal_valid")):
            marks[row:row + 1, 0:WS] = r_("small_" + name)[:, small]
            marks[row:row + 1, WS:LINE] = r_("large_" + name)[:, large]
        for row, count, name in ((0, 1, "depth"), (8, 3, "normals")):
            values[row:row + count, 0:WS] = r_("small_" + name)[:, small]
            values[row:row + count, WS:LINE] = r_("large_" + name)[:, large]

    for section in range(2):
        pl.when(s == section)(functools.partial(own_line, section))
    proj[...] = jnp.zeros(proj.shape, BF16)
    for task, (row, name) in enumerate(((0, "seg_proj"), (DEPTH_ROW, "depth_proj"), (NORMAL_ROW, "normal_proj"))):
        matrix = r_(name)[...]
        proj[row:row + matrix.shape[0], task * HEADW:(task + 1) * HEADW] = matrix
    xh = r_("xh")
    xh_slot = links.slots()
    pltpu.make_async_copy(x.at[:, pl.ds(pl.multiple_of(s * WIDE, WIDE), WIDE)], xh, links.recv.at[xh_slot]).start()
    pl.semaphore_wait(gate, total - 1)

    def plane_sum(key, width_of):
        near = r_(key + "a")
        count = near.shape[0]
        own = spot if count == 4 else 4 * s + spot
        first = links.slots(count)
        for bits in range(1, count):
            to = flip(own, bits)
            device = (s, 4 * plane + to) if count == 4 else (to // 4, 4 * plane + to % 4)
            links.put(near.at[own], near.at[own], device, first + bits)

        def finish():
            for bits in range(1, count):
                links.landed(near.at[flip(own, bits)], first + bits)
            acc = near[0]
            for index in range(1, count):
                acc = acc + near[index]
            return acc

        return finish

    def line_sum(key, value):
        far = r_(key + "b")
        far[plane] = value
        first, out = links.slots(planes), links.outs(planes)

        def make(offset):
            to = (plane + offset) % planes
            return links.copy(far.at[plane], far.at[plane], (s, 4 * to + spot), out + offset, first + offset)

        several(planes - 1, lambda i: make(i + 1).start())
        links.open.append(lambda: several(planes - 1, lambda i: make(i + 1).wait_send()))

        def finish():
            several(planes - 1, lambda i: links.landed(far.at[0], first + i + 1))
            acc = far[0]
            for index in range(1, planes):
                acc = acc + far[index]
            return acc

        return finish

    def add_up(key):
        return line_sum(key, plane_sum(key, None)())()

    def own_slot(key):
        near = r_(key + "a")
        return near.at[spot if near.shape[0] == 4 else 4 * s + spot]

    def put_stats(key, rows, first, second=None):
        slot = own_slot(key)
        slot[...] = jnp.zeros(slot.shape, F32)
        for group in range(2):
            a = b = None
            for g, rng in seg_rows(rows):
                if g == group:
                    one, two = first(g, rng), second(g, rng)
                    one, two = jnp.sum(one, axis=0, keepdims=True), jnp.sum(two, axis=0, keepdims=True)
                    a, b = (one, two) if a is None else (a + one, b + two)
            slot[2 * group:2 * group + 1, :] = a
            slot[2 * group + 1:2 * group + 2, :] = b

    counts = (2.0 * dp * WS, 2.0 * dp * WL)

    def moments(sums):
        means, invs = [], []
        for group in range(2):
            mean = sums[2 * group:2 * group + 1, :] / counts[group]
            var = sums[2 * group + 1:2 * group + 2, :] / counts[group] - mean * mean
            means.append(mean)
            invs.append(lax.rsqrt(var + EPS))
        return means, invs

    gathers = []
    if shape.inside:
        shards = (
            r_("reduce_w").at[:, pl.ds(pl.multiple_of(s * HALF, HALF), HALF)],
            r_("dilated_w").at[:, pl.ds(pl.multiple_of(s * HALF, HALF), HALF)],
            r_("expand_w").at[:, pl.ds(pl.multiple_of(s * WIDE, WIDE), WIDE)],
        )
        near_x, near_y, corner = flip(spot, 1), flip(spot, 2), flip(spot, 3)
        at_x, at_y = (s, 4 * plane + near_x), (s, 4 * plane + near_y)

        def gather(index):
            rows, wide = shape.rows[index], shape.wide[index]
            buf = r_(f"w{index}")
            cut = rows // 2
            first, out = links.slots(planes), links.outs(planes)
            mine = pltpu.make_async_copy(shards[index], buf.at[plane, spot], links.recv.at[first])
            mine.start()

            def make(offset):
                to = (plane + offset) % planes
                return links.copy(shards[index], buf.at[plane, spot], (s, 4 * to + spot), out + offset, first + offset)

            several(planes - 1, lambda i: make(i + 1).start())
            links.open.append(lambda: several(planes - 1, lambda i: make(i + 1).wait_send()))
            up, low = pl.ds(0, cut), pl.ds(cut, cut)
            slot = links.slots(6)
            yield
            mine.wait()
            several(planes - 1, lambda i: links.landed(buf.at[0, 0], first + i + 1))
            links.put(buf.at[:, spot, up], buf.at[:, spot, up], at_x, slot)
            links.put(buf.at[:, spot, low], buf.at[:, spot, low], at_y, slot + 1)
            links.put(buf.at[:, spot, up], buf.at[:, spot, up], at_y, slot + 2)
            links.put(buf.at[:, spot, low], buf.at[:, spot, low], at_x, slot + 3)
            yield
            links.landed(buf.at[:, near_x, up], slot)
            links.put(buf.at[:, near_x, up], buf.at[:, near_x, up], at_y, slot + 4)
            links.landed(buf.at[:, near_y, low], slot + 1)
            links.put(buf.at[:, near_y, low], buf.at[:, near_y, low], at_x, slot + 5)
            yield
            links.landed(buf.at[:, near_y, up], slot + 2)
            links.landed(buf.at[:, near_x, low], slot + 3)
            links.landed(buf.at[:, corner, up], slot + 4)
            links.landed(buf.at[:, corner, low], slot + 5)
            yield

        gathers = [gather(index) for index in range(3)]
        for one in gathers:
            next(one)
        weights = [r_(f"w{index}") for index in range(3)]
    else:
        weights = [r_("reduce_w"), r_("dilated_w"), r_("expand_w")]

    def gather_on(index):
        if shape.inside:
            next(gathers[index])

    kernel = r_("kernel")
    unit, halves = shape.unit, shape.units_half
    share = 2 * halves
    kernel_slot = links.slots(TAPS * halves)
    kernel_out = links.outs(TAPS * teams)

    def unit_at(index):
        number = TAPS * d + index
        tap, chunk = number // dp, number % dp
        inner = chunk % share
        return inner // halves == s, chunk // share, tap, inner % halves

    def kernel_copy(index, to_team):
        sends, to_rank, tap, place = unit_at(index)
        src = r_("head_w").at[index]
        dst = kernel.at[tap, s, pl.ds(pl.multiple_of(place * unit, unit), unit)]
        to = to_team * TEAM + to_rank
        slot = kernel_slot + tap * halves + place
        to_core = jnp.where(to == d, other, s)
        remote = lambda: links.copy(src, dst, (to_core, to), kernel_out + index * teams + to_team, slot)
        local = lambda: pltpu.make_async_copy(src, dst, links.recv.at[slot])
        return sends, to == d, remote, local

    def kernel_start(index, to_team):
        sends, mine, remote, local = kernel_copy(index, to_team)
        pl.when(sends & mine)(lambda: local().start())
        pl.when(sends & jnp.logical_not(mine))(lambda: remote().start())

    def kernel_done(index, to_team):
        sends, mine, remote, _ = kernel_copy(index, to_team)
        pl.when(sends & jnp.logical_not(mine))(lambda: remote().wait_send())

    def kernel_send():
        lax.fori_loop(0, TAPS * teams, lambda i, c: (kernel_start(i // teams, i % teams), c)[1], 0)

    links.open.append(lambda: lax.fori_loop(0, TAPS * teams, lambda i, c: (kernel_done(i // teams, i % teams), c)[1], 0))

    def same_image(block, tap_row):
        near = block + (tap_row - 1)
        inside = (near >= 0) & (near < dp)
        return [inside & ((2 * near + 2 * height) // height == (2 * block + 2 * height) // height) for height in HEIGHTS]

    def row_mask(block, tap_row, rows=PIX):
        small, large = [flag.astype(F32) for flag in same_image(block, tap_row)]
        return jnp.where(position(rows) < WS, small, large)

    def own_part(name, width):
        return r_(name)[0:1, pl.ds(pl.multiple_of(s * width, width), width)]

    norm1 = own_part("reduce_gain", HALF), own_part("reduce_bias", HALF)
    norm2 = own_part("dilated_gain", HALF), own_part("dilated_bias", HALF)
    norm3 = own_part("expand_gain", WIDE), own_part("expand_bias", WIDE)
    pre1, pre2, pre3 = r_("pre1"), r_("pre2"), r_("pre3")
    act1, act2 = r_("act1"), r_("act2")
    squares = lambda ref: (lambda g, rng: ref[rng, :], lambda g, rng: ref[rng, :] * ref[rng, :])

    gather_on(0)
    gather_on(0)
    gather_on(1)
    kernel_send()
    gather_on(0)
    pre1[...] = mm(x[...], take_rows(weights[0], 0, C))
    back_slot = links.slots()
    half_planes = planes // 2

    def rows_half(section):
        if shape.inside:
            return weights[0].at[pl.ds(pl.multiple_of(section * half_planes, half_planes), half_planes)]
        return weights[0].at[pl.ds(pl.multiple_of(section * WIDE, WIDE), WIDE)]

    links.put(rows_half(other), r_("wback"), partner, back_slot)
    put_stats("s1", 2, *squares(pre1))
    gather_on(1)
    gather_on(2)
    mean1, inv1 = moments(add_up("s1"))
    gain, bias = norm1
    for group, rng in seg_rows(2):
        hat = (pre1[rng, :] - mean1[group]) * inv1[group]
        pre1[rng, :] = hat
        act1[1, s, rng, :] = silu(hat * gain + bias).astype(BF16)
    slot = links.slots(5)
    above, below = jnp.maximum(d - 1, 0), jnp.minimum(d + 1, dp - 1)
    has_above, has_below = d > 0, d < dp - 1
    links.put(act1.at[1, s], act1.at[2, s], (s, above), slot + 1 + s, has_above)
    links.put(act1.at[1, s], act1.at[0, s], (s, below), slot + 3 + s, has_below)
    links.put(act1.at[1, s], act1.at[1, s], partner, slot)

    @pl.when(jnp.logical_not(has_above))
    def _():
        act1[0] = jnp.zeros(act1.shape[1:], BF16)

    @pl.when(jnp.logical_not(has_below))
    def _():
        act1[2] = jnp.zeros(act1.shape[1:], BF16)

    act1s, patch2 = r_("act1s"), r_("patch2")
    gather_on(2)

    def spread_rows(tap_row, half):
        value = act1[tap_row, half].astype(F32)
        if tap_row != 1 and shape.borders:
            value = value * row_mask(d, tap_row)
        for tap_col in range(3):
            piece = sideways(value, tap_col).astype(BF16)
            at = (3 * tap_row + tap_col) * BOT + half * HALF
            act1s[tap_col, tap_row, half] = piece
            patch2[:, at:at + HALF] = piece

    links.landed(act1.at[1, other], slot)
    for half in range(2):
        spread_rows(1, half)
    links.landed(act1.at[2, s], slot + 1 + s, has_below)
    links.put(act1.at[2, s], act1.at[2, s], partner, slot + 1 + s, has_below)
    links.landed(act1.at[0, s], slot + 3 + s, has_above)
    links.put(act1.at[0, s], act1.at[0, s], partner, slot + 3 + s, has_above)
    links.landed(act1.at[2, other], slot + 1 + other, has_below)
    for half in range(2):
        spread_rows(2, half)
    links.landed(act1.at[0, other], slot + 3 + other, has_above)
    for half in range(2):
        spread_rows(0, half)
    gather_on(1)
    pre2[...] = mm(patch2[...], take_rows(weights[1], 0, TAPS * BOT))
    put_stats("s2", 2, *squares(pre2))
    mean2, inv2 = moments(add_up("s2"))
    gain, bias = norm2
    for group, rng in seg_rows(2):
        hat = (pre2[rng, :] - mean2[group]) * inv2[group]
        pre2[rng, :] = hat
        act2[s, rng, :] = silu(hat * gain + bias).astype(BF16)
    slot = links.slots()
    links.put(act2.at[s], act2.at[s], partner, slot)
    gather_on(2)
    links.landed(act2.at[other], slot)
    pre3[...] = mm(act2[0], take_rows(weights[2], 0, HALF)) + mm(act2[1], take_rows(weights[2], HALF, HALF))
    put_stats("s3", 2, *squares(pre3))
    mean3, inv3 = moments(add_up("s3"))
    links.landed(xh, xh_slot)
    gain, bias = norm3
    outb = r_("outb")
    for group, rng in seg_rows(2):
        hat = (pre3[rng, :] - mean3[group]) * inv3[group]
        pre3[rng, :] = hat
        value = silu(hat * gain + bias + xh[rng, :].astype(F32)).astype(BF16)
        for part in range(4):
            for half in range(2):
                at = part * CH + half * (CH // 2)
                outb[part, half, rng, :] = value[:, at:at + CH // 2]
        start, length = SEGMENTS[group]
        line = rng.start // LINE
        whole = r_(("small_out_o", "large_out_o")[group])
        whole[line * length:(line + 1) * length, pl.ds(pl.multiple_of(s * WIDE, WIDE), WIDE)] = value

    outs = r_("outs")
    seat = rank // 4
    slot = links.slots(6)
    for part in range(4):
        to_rank = 4 * s + part
        src = outb.at[part]
        chip = team * TEAM + to_rank
        links.put_or_keep(src, outs.at[1, rank % 4 + 1], (seat, chip), slot + rank % 4 + 1, (seat == s) & (part == rank % 4))
    out_slot = links.slots(2)
    out_parts = [r_(name).at[:, pl.ds(pl.multiple_of(s * WIDE, WIDE), WIDE)] for name in ("small_out_o", "large_out_o")]
    for index, out_part in enumerate(out_parts):
        links.put(out_part, out_part, partner, out_slot + index)
    has_low = (s == 1) | (team > 0)
    has_high = (s == 0) | (team < teams - 1)

    @pl.when(jnp.logical_not(has_low))
    def _():
        outs[1, 0] = jnp.zeros((2, PIX, CH // 2), BF16)

    @pl.when(jnp.logical_not(has_high))
    def _():
        outs[1, 5] = jnp.zeros((2, PIX, CH // 2), BF16)

    near_block, near_border = 4 - 3 * s, 5 * s
    far_block, far_border = 1 + 3 * s, 5 - 5 * s
    far_chip = (other, jnp.clip(d + TEAM * (2 * s - 1), 0, dp - 1))
    has_far = (has_low & (s == 0)) | (has_high & (s == 1))
    for index in range(1, 5):
        links.landed(outs.at[1, index], slot + index)
    links.put(outs.at[1, near_block], outs.at[1, near_border], partner, slot + near_border)
    links.put(outs.at[1, far_block], outs.at[1, far_border], far_chip, slot + far_border, has_far)

    swap_slot = links.slots()
    several(TAPS * halves, lambda i: links.landed(kernel.at[0, 0, pl.ds(0, unit)], kernel_slot + i))
    links.put(kernel.at[:, s], kernel.at[:, s], partner, swap_slot)

    def widen(index, carry):
        for half in range(2):
            value = outs[1, index, half].astype(F32)
            outs[0, index, half] = sideways(value, 0).astype(BF16)
            outs[2, index, half] = sideways(value, 2).astype(BF16)
        return carry

    lax.fori_loop(1, 5, widen, 0)
    links.landed(kernel.at[:, other], swap_slot)

    first_block = team * TEAM + 4 * s
    patch, part, partm = r_("patch"), r_("part"), r_("partm")
    parts, partsm = r_("parts"), r_("partsm")
    part_slot = links.slots(2 * TEAM)

    def head_block(index):
        for tap_row in range(3):
            for tap_col in range(3):
                for half in range(2):
                    piece = outs[tap_col, index + tap_row, half]
                    if tap_row != 1 and shape.borders:
                        piece = piece * row_mask(first_block + index, tap_row).astype(BF16)
                    at = (3 * tap_row + tap_col) * CH + half * (CH // 2)
                    patch[:, at:at + CH // 2] = piece
        value = mm(patch[...], kernel[...].reshape(TAPS * CH, HEADS))
        for line in range(2):
            number = 2 * index + line
            for group, (start, length) in enumerate(SEGMENTS):
                rows = value[line * LINE + start:line * LINE + start + length, :]
                middle = jnp.mean(rows, axis=0, keepdims=True)
                partm[number, group:group + 1, :] = middle
                part[number, start:start + length, :] = (rows - middle).astype(BF16)
            chip = team * TEAM + 4 * s + index
            mine = (4 * s + index == rank) & (s == line)
            links.put_or_keep(part.at[number], parts.at[rank], (line, chip), part_slot + rank, mine)
            links.put_or_keep(partm.at[number], partsm.at[rank], (line, chip), part_slot + TEAM + rank, mine)

    head_block(1)
    head_block(2)
    links.landed(outs.at[1, 0], slot, has_low)
    links.landed(outs.at[1, 5], slot + 5, has_high)
    widen(0, 0)
    widen(5, 0)
    head_block(0)
    head_block(3)

    for index in range(TEAM):
        links.landed(parts.at[index], part_slot + index)
        links.landed(partsm.at[index], part_slot + TEAM + index)
    preh, acth, dyh = r_("preh"), r_("acth"), r_("dyh")
    for group, (start, length) in enumerate(SEGMENTS):
        rng = slice(start, start + length)
        acc = sum(parts[index, rng, :].astype(F32) for index in range(TEAM))
        acc = acc + sum(partsm[index, group:group + 1, :] for index in range(TEAM))
        preh[rng, :] = acc

    labels, depth, normals = marks[0:1, :], values[0:1, :], values[8:11, :]
    seg_keep = (labels >= 0).astype(F32)
    depth_keep, normal_keep = marks[1:2, :].astype(F32), marks[2:3, :].astype(F32)
    lane = lax.broadcasted_iota(jnp.int32, (1, LINE), 1)
    small_lane = lane < WS
    put_stats("sh", 1, *squares(preh))
    slot_ref = own_slot("sh")
    tally = jnp.zeros((1, LINE), F32)
    for number, keep in enumerate((seg_keep, depth_keep, normal_keep)):
        for group in range(2):
            count = jnp.sum(jnp.where(small_lane == (group == 0), keep, 0.0), axis=1, keepdims=True)
            tally = tally + jnp.where(lane == 2 * number + group, count, 0.0)
    slot_ref[4:5, 0:LINE] = tally
    sums = add_up("sh")
    meanh, invh = moments(sums)
    tally = sums[4:5, 0:LINE]

    def pixel_count(number):
        picked = [jnp.sum(jnp.where(lane == 2 * number + group, tally, 0.0), axis=1, keepdims=True) for group in range(2)]
        return jnp.maximum(jnp.where(small_lane, picked[0], picked[1]), 1.0)

    gain, bias = head_norm[0:1, :], head_norm[1:2, :]
    for group, rng in seg_rows(1):
        hat = (preh[rng, :] - meanh[group]) * invh[group]
        preh[rng, :] = hat
        acth[rng, :] = silu(hat * gain + bias).astype(BF16)

    scores = mm(proj[...], acth[...], NT)
    row = lax.broadcasted_iota(jnp.int32, (16, LINE), 0)
    logits = jnp.where(row < NCLS, scores[0:16, :], -1e30)
    top = jnp.max(logits, axis=0, keepdims=True)
    power = jnp.where(row < NCLS, jnp.exp(logits - top), 0.0)
    soft = power / jnp.sum(power, axis=0, keepdims=True)
    onehot = (row == labels).astype(F32)
    d_logits = (soft - onehot) * (seg_keep / pixel_count(0))
    gap = scores[DEPTH_ROW:DEPTH_ROW + 1, :] - depth
    d_depth = depth_keep / pixel_count(1) * gap * lax.rsqrt(gap * gap + 1.0)
    guess = scores[NORMAL_ROW:NORMAL_ROW + 3, :]
    inverse = lax.rsqrt(jnp.sum(guess * guess, axis=0, keepdims=True) + 1.0)
    along = jnp.sum(guess * normals, axis=0, keepdims=True)
    weight = normal_keep / pixel_count(2)
    d_guess = r_("dscore")
    d_guess[...] = jnp.zeros(d_guess.shape, F32)
    d_guess[0:16, :] = d_logits
    d_guess[DEPTH_ROW:DEPTH_ROW + 1, :] = d_depth
    d_guess[NORMAL_ROW:NORMAL_ROW + 3, :] = -weight * (normals * inverse - along * (inverse * inverse * inverse) * guess)
    d_scores = d_guess[...]
    high = d_scores.astype(BF16)
    low = (d_scores - high.astype(F32)).astype(BF16)
    d_act = mm(high, proj[...], TN) + mm(low, proj[...], TN)
    value = mm(high, acth[...]) + mm(low, acth[...])
    d_proj = r_("dproj")
    d_proj[0:16, :] = value[0:16, 0:HEADW]
    d_proj[16:24, :] = value[16:24, HEADW:2 * HEADW]
    d_proj[24:32, :] = value[24:32, 2 * HEADW:]
    for group, rng in seg_rows(1):
        dyh[rng, :] = d_act[rng, :] * slope(preh[rng, :] * gain + bias)
    put_stats("th", 1, lambda g, rng: dyh[rng, :], lambda g, rng: dyh[rng, :] * preh[rng, :])
    sums = add_up("th")
    r_("head_vec_o")[...] = sums
    dph, dpx = r_("dph"), r_("dpx")
    for group, rng in seg_rows(1):
        first, second = sums[2 * group:2 * group + 1, :], sums[2 * group + 1:2 * group + 2, :]
        value = dyh[rng, :] - first / counts[group] - preh[rng, :] * (second / counts[group])
        dph[rng, :] = (gain * invh[group] * value).astype(BF16)

    slot = links.slots(12)
    place = rank % 4 + 1
    for step in range(TEAM):
        chip = team * TEAM + flip(rank, step)
        if step == 0:
            links.put_or_keep(dph, dpx.at[place, s], (seat, chip), slot + 2 * place + s, seat == s)
        else:
            links.put(dph, dpx.at[place, s], (seat, chip), slot + 2 * place + s)

    @pl.when(jnp.logical_not(has_low))
    def _():
        dpx[0] = jnp.zeros((2, LINE, HEADS), BF16)

    @pl.when(jnp.logical_not(has_high))
    def _():
        dpx[5] = jnp.zeros((2, LINE, HEADS), BF16)

    for index in range(2, 10):
        links.landed(dpx.at[index // 2, index % 2], slot + index)
    links.put(dpx.at[near_block], dpx.at[near_border], partner, slot + 2 * near_border)
    links.put(dpx.at[far_block], dpx.at[far_border], far_chip, slot + 2 * far_border, has_far)
    links.landed(dpx.at[0], slot, has_low)
    links.landed(dpx.at[5], slot + 10, has_high)

    dks, dkr, dku, dkg = r_("dks"), r_("dkr"), r_("dku"), r_("dkg")

    def tap_grad(tap, half):
        tap_row, tap_col = tap // 3, tap % 3
        acc = None
        for index in range(4):
            left = outs[tap_col, index + tap_row, half]
            right = dpx[index + 1].reshape(PIX, HEADS)
            if shape.borders:
                right = right * row_mask(first_block + index, tap_row).astype(BF16)
            term = mm(left, right, TN)
            acc = term if acc is None else acc + term
        return acc

    def their_tap(tap, carry):
        dks[tap] = tap_grad(tap, other).astype(BF16)
        return carry

    lax.fori_loop(0, TAPS, their_tap, 0)
    swap_slot = links.slots()
    links.put(dks, dkr, partner, swap_slot)

    dps, grads = r_("dps"), r_("grads")
    for task in range(3):
        cols = slice(task * HEADW, (task + 1) * HEADW)

        def spread(index, carry):
            piece = dpx[index, :, :, cols].reshape(PIX, HEADW)
            value = piece.astype(F32)
            dps[1, index] = piece
            dps[0, index] = sideways(value, 0).astype(BF16)
            dps[2, index] = sideways(value, 2).astype(BF16)
            return carry

        lax.fori_loop(0, 6, spread, 0)

        def pull(index, carry):
            acc = None
            for tap_row in range(3):
                for tap_col in range(3):
                    piece = dps[tap_col, index + tap_row]
                    if tap_row != 1 and shape.borders:
                        piece = piece * row_mask(first_block + index, tap_row).astype(BF16)
                    tap = 8 - (3 * tap_row + tap_col)
                    term = mm(piece, kernel[tap, :, :, cols].reshape(CH, HEADW), NT)
                    acc = term if acc is None else acc + term
            grads[task, index] = acc
            return carry

        lax.fori_loop(0, 4, pull, 0)

    pairs = [(i, j) for i in range(3) for j in range(i, 3)]

    def dots(index, sums):
        sums = list(sums)
        for group, rng in seg_rows(2):
            block = [grads[task, index, rng, :] for task in range(3)]
            for number, (i, j) in enumerate(pairs):
                sums[6 * group + number] += jnp.sum(block[i] * block[j], axis=0, keepdims=True)
        return tuple(sums)

    sums = lax.fori_loop(0, 4, dots, (jnp.zeros((1, CH), F32),) * (2 * len(pairs)))
    slot_ref = own_slot("gm")
    slot_ref[0:16, :] = jnp.zeros((16, HEADW), F32)
    for number, total_row in enumerate(sums):
        slot_ref[number:number + 1, :] = total_row
    slot_ref[16:, :] = d_proj[...]
    near_done = plane_sum("gm", None)

    def my_tap(tap, carry):
        dku[tap] = tap_grad(tap, s).astype(BF16)
        return carry

    lax.fori_loop(0, TAPS, my_tap, 0)
    links.landed(dkr, swap_slot)

    def both(tap, carry):
        dku[tap] = (dku[tap].astype(F32) + dkr[tap].astype(F32)).astype(BF16)
        return carry

    lax.fori_loop(0, TAPS, both, 0)

    grad_slot = links.slots(teams * TAPS)
    grad_out = links.outs(TAPS * halves)

    def grad_copy(number):
        tap, place = number // halves, number % halves
        chunk = rank * share + s * halves + place
        overall = tap * dp + chunk
        owner, index = overall // TAPS, overall % TAPS
        src = dku.at[tap, pl.ds(pl.multiple_of(place * unit, unit), unit)]
        dst = dkg.at[team, index]
        at = grad_slot + team * TAPS + index
        to_core = jnp.where(owner == d, other, s)
        remote = lambda: links.copy(src, dst, (to_core, owner), grad_out + number, at)
        local = lambda: pltpu.make_async_copy(src, dst, links.recv.at[at])
        return owner == d, remote, local

    def grad_start(number):
        mine, remote, local = grad_copy(number)
        pl.when(mine)(lambda: local().start())
        pl.when(jnp.logical_not(mine))(lambda: remote().start())

    def grad_done(number):
        mine, remote, _ = grad_copy(number)
        pl.when(jnp.logical_not(mine))(lambda: remote().wait_send())

    lax.fori_loop(0, TAPS * halves, lambda i, c: (grad_start(i), c)[1], 0)
    links.open.append(lambda: lax.fori_loop(0, TAPS * halves, lambda i, c: (grad_done(i), c)[1], 0))

    far_done = line_sum("gm", near_done())
    gram_rows = far_done()
    r_("proj_o")[...] = gram_rows[16:, :]
    dot_of = jnp.sum(gram_rows[0:16, :], axis=1, keepdims=True)
    gram = {
        pair: jnp.where(lane == 0, dot_of[k:k + 1, :], dot_of[6 + k:7 + k, :]) for k, pair in enumerate(pairs)
    }
    alphas = jacobi_weights(gram)
    alphas = [[alpha[:, group:group + 1] for alpha in alphas] for group in range(2)]

    doutb, dout = r_("doutb"), r_("dout")
    slot = links.slots(4)
    for index in range(4):
        for group, rng in seg_rows(2):
            aligned = sum(alphas[group][task] * grads[task, index, rng, :] for task in range(3))
            doutb[index, rng, :] = aligned.astype(BF16)
        chip = team * TEAM + 4 * s + index
        links.put_or_keep(
            doutb.at[index], dout.at[rank % 4], (seat, chip), slot + rank % 4, (seat == s) & (rank % 4 == index)
        )

    for index in range(4):
        links.landed(dout.at[index], slot + index)
    du, dpre3 = r_("du"), r_("dpre3")
    gain, bias = norm3
    for group, rng in seg_rows(2):
        at = slope(pre3[rng, :] * gain + bias + xh[rng, :].astype(F32))
        for part_index in range(4):
            cols = slice(part_index * CH, (part_index + 1) * CH)
            du[rng, cols] = dout[part_index, rng, :].astype(F32) * at[:, cols]
    vec = r_("vec_o")
    with_hat = lambda dy, hat: (lambda g, rng: dy[rng, :], lambda g, rng: dy[rng, :] * hat[rng, :])
    put_stats("t3", 2, *with_hat(du, pre3))
    sums = add_up("t3")
    vec[s, 0:1, :] = sums[1:2, :] + sums[3:4, :]
    vec[s, 1:2, :] = sums[0:1, :] + sums[2:3, :]

    def norm_back(sums, group, rng, dy, hat, scale):
        first, second = sums[2 * group:2 * group + 1, :], sums[2 * group + 1:2 * group + 2, :]
        return scale * (dy[rng, :] - first / counts[group] - hat[rng, :] * (second / counts[group]))

    for group, rng in seg_rows(2):
        dpre3[rng, :] = norm_back(sums, group, rng, du, pre3, gain * inv3[group]).astype(BF16)
    half2, half2r = r_("half2"), r_("half2r")
    value = mm(dpre3[...], take_rows(weights[2], 0, BOT), NT)
    half2[0], half2[1] = value[:, :HALF], value[:, HALF:]
    slot = links.slots()
    links.put(half2.at[other], half2r, partner, slot)

    def scatter(index):
        rows, wide = shape.rows[index], shape.wide[index]
        cut = rows // 2
        up, low = pl.ds(0, cut), pl.ds(cut, cut)
        buf = r_(f"dw{index}")
        ra, rb, rc = r_(f"ra{index}"), r_(f"rb{index}"), r_(f"rc{index}")
        slot = links.slots(6)
        links.put(buf.at[:, near_y, up], ra.at[0, :, 0], at_y, slot)
        links.put(buf.at[:, corner, up], ra.at[0, :, 1], at_y, slot + 1)
        links.put(buf.at[:, near_x, low], ra.at[1, :, 0], at_x, slot + 2)
        links.put(buf.at[:, corner, low], ra.at[1, :, 1], at_x, slot + 3)
        yield

        def add(at, part, extra):
            total = buf[:, at, part].astype(F32) + extra.astype(F32)
            buf[:, at, part] = total.astype(BF16)

        links.landed(ra.at[0, :, 1], slot + 1)
        add(near_x, up, ra[0, :, 1])
        links.put(buf.at[:, near_x, up], rb.at[0], at_x, slot + 4)
        links.landed(ra.at[1, :, 1], slot + 3)
        add(near_y, low, ra[1, :, 1])
        links.put(buf.at[:, near_y, low], rb.at[1], at_y, slot + 5)
        yield
        links.landed(ra.at[0, :, 0], slot)
        links.landed(ra.at[1, :, 0], slot + 2)
        links.landed(rb.at[0], slot + 4)
        add(spot, up, ra[0, :, 0].astype(F32) + rb[0].astype(F32))
        links.landed(rb.at[1], slot + 5)
        add(spot, low, ra[1, :, 0].astype(F32) + rb[1].astype(F32))
        first, out = links.slots(planes), links.outs(planes)

        def make(offset):
            to = (plane + offset) % planes
            return links.copy(buf.at[to, spot], rc.at[plane], (s, 4 * to + spot), out + offset, first + offset)

        several(planes - 1, lambda i: make(i + 1).start())
        links.open.append(lambda: several(planes - 1, lambda i: make(i + 1).wait_send()))
        rc[plane] = buf[plane, spot]
        yield
        several(planes - 1, lambda i: links.landed(rc.at[0], first + i + 1))
        acc = rc[0].astype(F32)
        for number in range(1, planes):
            acc = acc + rc[number].astype(F32)
        result = r_(f"dw{index}_o")
        mine = pl.ds(pl.multiple_of(s * wide, wide), wide)
        result[:, mine] = acc.astype(BF16)
        at = links.slots()
        links.put(result.at[:, mine], result.at[:, mine], partner, at)
        yield
        links.landed(result.at[:, mine], at)
        yield

    def advance(one):
        if one is not None:
            next(one)

    def reduced(index):
        if not shape.inside:
            return None
        one = scatter(index)
        next(one)
        return one

    grad_of = lambda index: r_(f"dw{index}") if shape.inside else r_(f"dw{index}_o")
    for half in range(2):
        put_rows(grad_of(2), half * HALF, mm(act2[half], dpre3[...], TN).astype(BF16))
    third = reduced(2)

    links.landed(half2r, slot)
    dy2, dp2 = r_("dy2"), r_("dp2")
    gain, bias = norm2
    for group, rng in seg_rows(2):
        value = half2[s, rng, :] + half2r[rng, :]
        dy2[rng, :] = value * slope(pre2[rng, :] * gain + bias)
    put_stats("t2", 2, *with_hat(dy2, pre2))
    advance(third)
    sums = add_up("t2")
    vec[s, 2:3, 0:HALF] = sums[1:2, :] + sums[3:4, :]
    vec[s, 2:3, HALF:2 * HALF] = sums[0:1, :] + sums[2:3, :]
    for group, rng in seg_rows(2):
        dp2[1, rng, :] = norm_back(sums, group, rng, dy2, pre2, gain * inv2[group]).astype(BF16)
    slot = links.slots(2)
    links.put(dp2.at[1], dp2.at[2], (s, above), slot, has_above)
    links.put(dp2.at[1], dp2.at[0], (s, below), slot + 1, has_below)

    @pl.when(jnp.logical_not(has_above))
    def _():
        dp2[0] = jnp.zeros((PIX, HALF), BF16)

    @pl.when(jnp.logical_not(has_below))
    def _():
        dp2[2] = jnp.zeros((PIX, HALF), BF16)

    for tap in range(TAPS):
        for half in range(2):
            at = tap * BOT + half * HALF
            put_rows(grad_of(1), at, mm(act1s[tap % 3, tap // 3, half], dp2[1], TN).astype(BF16))
    second = reduced(1)
    advance(third)
    links.landed(dp2.at[2], slot, has_below)
    links.landed(dp2.at[0], slot + 1, has_above)
    acc = None
    for tap_row in range(3):
        value = dp2[tap_row].astype(F32)
        if tap_row != 1 and shape.borders:
            value = value * row_mask(d, tap_row)
        for tap_col in range(3):
            tap = 8 - (3 * tap_row + tap_col)
            term = mm(sideways(value, tap_col).astype(BF16), take_rows(weights[1], tap * BOT, BOT), NT)
            acc = term if acc is None else acc + term
    half1, half1r = r_("half1"), r_("half1r")
    half1[0], half1[1] = acc[:, :HALF], acc[:, HALF:]
    slot = links.slots()
    links.put(half1.at[other], half1r, partner, slot)
    advance(second)
    links.landed(half1r, slot)
    dy1, dp1 = r_("dy1"), r_("dp1")
    gain, bias = norm1
    for group, rng in seg_rows(2):
        value = half1[s, rng, :] + half1r[rng, :]
        dy1[rng, :] = value * slope(pre1[rng, :] * gain + bias)
    put_stats("t1", 2, *with_hat(dy1, pre1))
    sums = add_up("t1")
    vec[s, 2:3, 2 * HALF:3 * HALF] = sums[1:2, :] + sums[3:4, :]
    vec[s, 2:3, 3 * HALF:4 * HALF] = sums[0:1, :] + sums[2:3, :]
    vec[s, 3:8, :] = jnp.zeros((5, WIDE), F32)
    vec_slot = links.slots()
    links.put(vec.at[s], vec.at[s], partner, vec_slot)
    for group, rng in seg_rows(2):
        dp1[s, rng, :] = norm_back(sums, group, rng, dy1, pre1, gain * inv1[group]).astype(BF16)
    slot = links.slots()
    links.put(dp1.at[s], dp1.at[s], partner, slot)
    for part_index in range(4):
        cols = slice(part_index * BOT, (part_index + 1) * BOT)
        put_rows(grad_of(0), part_index * BOT, mm(x[:, cols], dp1[s], TN).astype(BF16))
    first = reduced(0)
    advance(second)
    advance(third)

    links.landed(r_("wback"), back_slot)
    links.landed(dp1.at[other], slot)
    value = mm(dp1[s], rows_half(s)[...].reshape(WIDE, HALF), NT)
    value = value + mm(dp1[other], r_("wback")[...].reshape(WIDE, HALF), NT) + du[...]
    for line in range(2):
        r_("small_grad_o")[line * WS:(line + 1) * WS, :] = value[line * LINE:line * LINE + WS, :]
        r_("large_grad_o")[line * WL:(line + 1) * WL, :] = value[line * LINE + WS:(line + 1) * LINE, :]
    advance(first)
    advance(second)
    advance(first)

    result = r_("dk_o")
    done_slot, done_out = links.slots(TAPS), links.outs(TAPS)

    def finish_unit(index):
        mine, _, _, _ = unit_at(index)
        final = lambda: links.copy(result.at[index], result.at[index], partner, done_out + index, done_slot + index)

        @pl.when(mine)
        def _():
            several(teams, lambda t: links.landed(dkg.at[0, 0], grad_slot + t * TAPS + index))
            acc = dkg[0, index].astype(F32)
            for number in range(1, teams):
                acc = acc + dkg[number, index].astype(F32)
            result[index] = acc.astype(BF16)
            final().start()

        return mine, final

    lax.fori_loop(0, TAPS, lambda i, c: (finish_unit(i), c)[1], 0)

    def finished(index):
        mine, _, _, _ = unit_at(index)
        final = links.copy(result.at[index], result.at[index], partner, done_out + index, done_slot + index)
        pl.when(mine)(lambda: final.wait_send())
        pl.when(jnp.logical_not(mine))(lambda: links.landed(result.at[index], done_slot + index))

    advance(first)
    advance(first)
    advance(second)
    advance(third)
    lax.fori_loop(0, TAPS, lambda i, c: (finished(i), c)[1], 0)
    links.landed(vec.at[other], vec_slot)
    for index, out_part in enumerate(out_parts):
        links.landed(out_part, out_slot + index)
    links.close()
    used["send"], used["recv"] = links.used_send, links.used_recv


def body(
    reduce_weight,
    dilated_weight,
    expand_weight,
    reduce_gain,
    reduce_bias,
    dilated_gain,
    dilated_bias,
    expand_gain,
    expand_bias,
    head_conv,
    head_gain,
    head_bias,
    seg_proj,
    depth_proj,
    normal_proj,
    small_feats,
    small_labels,
    small_depth,
    small_normals,
    small_depth_valid,
    small_normal_valid,
    large_feats,
    large_labels,
    large_depth,
    large_normals,
    large_depth_valid,
    large_normal_valid,
):
    dp = lax.axis_size("dp")
    section = lax.axis_index("section")
    assert small_feats.shape[0] == 2 * WS and large_feats.shape[0] == 2 * WL
    shape = Shapes(dp)

    if not shape.inside:
        def whole(shard, wide):
            mine = lax.dynamic_slice_in_dim(shard, section * wide, wide, 1)
            return lax.all_gather(mine, "dp", axis=0, tiled=True)

        reduce_weight = whole(reduce_weight, HALF)
        dilated_weight = whole(dilated_weight, HALF)
        expand_weight = whole(expand_weight, WIDE)

    vmem = pl.BlockSpec(memory_space=pltpu.VMEM)
    anywhere = pl.BlockSpec(memory_space=pl.ANY)
    flat = lambda value: value.reshape(1, -1)
    inputs = {
        "reduce_w": reduce_weight,
        "dilated_w": dilated_weight,
        "expand_w": expand_weight,
        "head_w": head_conv.reshape(TAPS, shape.unit, HEADS),
        "reduce_gain": flat(reduce_gain),
        "reduce_bias": flat(reduce_bias),
        "dilated_gain": flat(dilated_gain),
        "dilated_bias": flat(dilated_bias),
        "expand_gain": flat(expand_gain),
        "expand_bias": flat(expand_bias),
        "head_gain": head_gain.reshape(-1, 128),
        "head_bias": head_bias.reshape(-1, 128),
        "seg_proj": seg_proj.T,
        "depth_proj": depth_proj.T,
        "normal_proj": normal_proj.T,
        "small_feats": small_feats,
        "small_labels": flat(small_labels),
        "small_depth": flat(small_depth),
        "small_normals": small_normals,
        "small_depth_valid": flat(small_depth_valid),
        "small_normal_valid": flat(small_normal_valid),
        "large_feats": large_feats,
        "large_labels": flat(large_labels),
        "large_depth": flat(large_depth),
        "large_normals": large_normals,
        "large_depth_valid": flat(large_depth_valid),
        "large_normal_valid": flat(large_normal_valid),
    }
    outputs = {
        "small_out_o": ((2 * WS, C), BF16),
        "large_out_o": ((2 * WL, C), BF16),
        "small_grad_o": ((2 * WS, WIDE), F32),
        "large_grad_o": ((2 * WL, WIDE), F32),
        "dk_o": ((TAPS, shape.unit, HEADS), BF16),
        "vec_o": ((2, 8, WIDE), F32),
        "head_vec_o": ((8, HEADS), F32),
        "proj_o": ((PROJ, HEADW), F32),
    }
    for index in range(3):
        if shape.inside:
            outputs[f"dw{index}_o"] = ((shape.rows[index], 2 * shape.wide[index]), BF16)
        else:
            outputs[f"dw{index}_o"] = ((shape.full[index], shape.wide[index]), BF16)
    scratch = scratch_of(shape)
    scratch["dscore"] = ((PROJ, LINE), F32)
    names = [*inputs, *outputs, *scratch, "send", "recv"]
    used = {}

    def call(room, *operands):
        return pl.pallas_call(
            functools.partial(fused, shape, names, used),
            out_shape=[jax.ShapeDtypeStruct(dims, kind) for dims, kind in outputs.values()],
            in_specs=[anywhere if name == "head_w" else vmem for name in inputs],
            out_specs=[vmem] * len(outputs),
            scratch_shapes=[pltpu.VMEM(dims, kind) for dims, kind in scratch.values()]
            + [pltpu.SemaphoreType.DMA((count,)) for count in room],
            compiler_params=pltpu.CompilerParams(
                collective_id=0, has_side_effects=True, vmem_limit_bytes=64 * 2**20 - 2**16
            ),
            name="fused",
        )(*operands)

    jax.eval_shape(functools.partial(call, (2048, 2048)), *inputs.values())
    got = dict(zip(outputs, call((used["send"], used["recv"]), *inputs.values())))
    if not shape.inside:
        for index in range(3):
            mine = lax.psum_scatter(got[f"dw{index}_o"].astype(F32), "dp", scatter_dimension=0, tiled=True)
            both = lax.all_gather(mine, "section", axis=0)
            got[f"dw{index}_o"] = both.transpose(1, 0, 2).reshape(shape.rows[index], -1)

    results = {
        "small_out": ((2 * WS, C), BF16),
        "large_out": ((2 * WL, C), BF16),
        "small_grad": ((2 * WS, WIDE), F32),
        "large_grad": ((2 * WL, WIDE), F32),
        "dw0": ((shape.rows[0], BOT), F32),
        "dw1": ((shape.rows[1], BOT), F32),
        "dw2": ((shape.rows[2], C), F32),
        "reduce_gain": ((1, BOT), F32),
        "reduce_bias": ((1, BOT), F32),
        "dilated_gain": ((1, BOT), F32),
        "dilated_bias": ((1, BOT), F32),
        "expand_gain": ((1, C), F32),
        "expand_bias": ((1, C), F32),
        "dk": ((TAPS * shape.unit, HEADS), F32),
        "head_gain": ((HEADS // 128, 128), F32),
        "head_bias": ((HEADS // 128, 128), F32),
        "seg_proj": ((NCLS, HEADW), F32),
        "depth_proj": ((1, HEADW), F32),
        "normal_proj": ((3, HEADW), F32),
    }
    final = pl.pallas_call(
        functools.partial(finish, [*got, *results]),
        out_shape=[jax.ShapeDtypeStruct(dims, kind) for dims, kind in results.values()],
        in_specs=[vmem] * len(got),
        out_specs=[vmem] * len(results),
        compiler_params=pltpu.CompilerParams(vmem_limit_bytes=64 * 2**20 - 2**16),
        name="finish",
    )(*got.values())
    vectors = ("gain", "bias")
    return tuple(
        value.reshape(-1) if name.endswith(vectors) else value.T if name.endswith("proj") else value
        for name, value in zip(results, final)
    )


def finish(names, *refs):
    env = dict(zip(names, refs))
    for name in ("small_out", "large_out", "small_grad", "large_grad"):
        env[name][...] = env[name + "_o"][...]
    for index in range(3):
        env[f"dw{index}"][...] = env[f"dw{index}_o"][...].astype(F32)
    taps, unit, _ = env["dk_o"].shape
    for tap in range(taps):
        env["dk"][tap * unit:(tap + 1) * unit, :] = env["dk_o"][tap].astype(F32)
    vec, head_vec = env["vec_o"], env["head_vec_o"]
    for section in range(2):
        for row, name in enumerate(("expand_gain", "expand_bias")):
            env[name][0:1, section * WIDE:(section + 1) * WIDE] = vec[section, row:row + 1, :]
        for part, name in enumerate(("dilated_gain", "dilated_bias", "reduce_gain", "reduce_bias")):
            env[name][0:1, section * HALF:(section + 1) * HALF] = vec[section, 2:3, part * HALF:(part + 1) * HALF]
    gain = head_vec[1:2, :] + head_vec[3:4, :]
    bias = head_vec[0:1, :] + head_vec[2:3, :]
    for part in range(HEADS // 128):
        cols = slice(part * 128, (part + 1) * 128)
        env["head_gain"][part:part + 1, :] = gain[:, cols]
        env["head_bias"][part:part + 1, :] = bias[:, cols]
    proj = env["proj_o"]
    env["seg_proj"][...] = proj[0:NCLS, :]
    env["depth_proj"][...] = proj[DEPTH_ROW:DEPTH_ROW + 1, :]
    env["normal_proj"][...] = proj[NORMAL_ROW:NORMAL_ROW + 3, :]


def solution(mesh):
    rows, vector = P("dp", None), P()
    pixels, parts = P("dp"), P(None, "dp")
    group = (rows, pixels, pixels, parts, pixels, pixels)
    in_specs = (rows, rows, rows) + (vector,) * 6 + (rows,) + (vector,) * 5 + group + group
    out_specs = (
        (rows, rows, P("dp", "section"), P("dp", "section"), rows, rows, rows)
        + (vector,) * 6
        + (rows,)
        + (vector,) * 5
    )
    return jax.shard_map(body, mesh=mesh, in_specs=in_specs, out_specs=out_specs, check_vma=False)
```

time: 2020 us -> 352 us (0.17)
  waiting for transfers between devices: 751 us -> 0 us
  blocking collectives: 438 us -> 0 us
  Pallas kernels: 0 us -> 351 us
  matrix products: 249 us -> 0 us
  local copies, waits for them, and re-layouts: 190 us -> 0 us
  starting transfers between devices: 145 us -> 0 us
  other arithmetic: 118 us -> 0 us
  between operations: 114 us -> 0.84 us
    psum x9 -> x0, blocking collectives: 438 us -> none  [the longest x6 285 us: block_moments(): return lax.psum((values[0], values[1]), 'dp')]
    reduce_scatter x4 -> x0, waiting for transfers between devices: 372 us -> none  [the longest x1 173 us: block_reduce(): lax.psum_scatter(grads[1], 'dp', scatter_dimension=0, tiled=True)]
    pallas_call x0 -> x2, Pallas kernels: none -> 351 us  [the longest x1 346 us: call(): pl.pallas_call(functools.partial(fused, shape, names, used), out_shape=[j...]
    all_gather x4 -> x0, waiting for transfers between devices: 301 us -> none  [the longest x1 181 us: body(): kernel = lax.all_gather(head_conv, 'dp', axis=0, tiled=True)]
    dot_general x44 -> x0, matrix products: 249 us -> none  [the longest x2 59.8 us: head_step(): lax.dot_general(patches, grad_pre, CONTRACT_ROWS, preferred_element_type=...]
    ppermute x37 -> x0, starting transfers between devices: 145 us -> none  [the longest x21 110 us: shifted(): return lax.ppermute(block, axis, route)]
    ppermute x37 -> x0, waiting for transfers between devices: 75.6 us -> none  [the longest x8 41.5 us: extended_2(): before = lax.ppermute(last, axis, up)]
    reshape x1 -> x0, local copies, waits for them, and re-layouts: 61.8 us -> none  [head_step(): kernel.reshape(9, C, 3, HEADW)]
  transfers between devices with their start and end apart: 45 -> 0, of which waited for: 15 -> 0; matrix products, arithmetic and copies ran while one was open for 21% -> 0% of each run, Pallas kernels for 0% -> 0%
where the time goes in v1:
time: 352 us
  Pallas kernels  351 us (100%)
    pallas_call x1, Pallas kernels, call(): pl.pallas_call(functools.partial(fused, shape, names, used), out_shape=[j...  346 us

profile of v1, /device:TPU:1, one launch (start us, length us, event | category | flops | bytes accessed | tf_op | source)
XLA Modules:
  0.0 351.6 jit_solution(10176872971432985346)
XLA Ops:
  0.7 345.6 %fused.1 = (bf16[96,2048]{1,0:T(8,128)(2,1)}, bf16[160,2048]{1,0:T(8,128)(2,1)}, f32[96,1024]{1,0:T(8,128)}, f32[160,1024]{1,0:T(8,128)}, bf16[9,128,768]{2,1,0:...) custom-call(bf16[128,512]{1,0:T(8,128)(2,1)} %refs_0_.1, ...), custom_call_target="tpu_custom_call" | custom-call | tf_op jit(solution)/shard_map/fused/pallas_call | solution.py:1267
  346.2 5.2 %finish.1 = (bf16[96,2048]{1,0:T(8,128)(2,1)}, bf16[160,2048]{1,0:T(8,128)(2,1)}, f32[96,1024]{1,0:T(8,128)}, f32[160,1024]{1,0:T(8,128)}, f32[128,512]{1,0:T(8,...) custom-call(bf16[96,2048]{1,0:T(8,128)(2,1)} %get-tuple-element.49.r, ...), custom_call_target="tpu_custom_call" | custom-call | tf_op jit(solution)/shard_map/finish/pallas_call | solution.py:1309

commit v2 on v1

--- a/solution.py
+++ b/solution.py
@@ -280,6 +280,7 @@
         "dku": ((TAPS, CH // 2, HEADS), BF16),
         "dproj": ((PROJ, HEADW), F32),
         "head_norm": ((8, HEADS), F32),
+        "tallies": ((4, LINE), F32),
         "marks": ((8, LINE), jnp.int32),
         "values": ((16, LINE), F32),
         "proj": ((PROJ, HEADS), BF16),
@@ -289,10 +290,12 @@
         ("s1", 4, HALF), ("s2", 4, HALF), ("s3", 4, WIDE), ("t3", 4, WIDE), ("t2", 4, HALF), ("t1", 4, HALF),
         ("sh", 8, HEADS), ("th", 8, HEADS),
     ):
-        table[name + "a"] = ((count, 8, width), F32)
-        table[name + "b"] = ((planes, 8, width), F32)
-    table["gma"] = ((8, 16 + PROJ, HEADW), F32)
-    table["gmb"] = ((planes, 16 + PROJ, HEADW), F32)
+        rows = 8 if name == "s1" else 4
+        table[name + "a"] = ((count, rows, width), F32)
+        table[name + "b"] = ((planes, rows, width), F32)
+    for name, rows, width in (("gm", 8, 128), ("pj", PROJ, HEADW)):
+        table[name + "a"] = ((8, rows, width), F32)
+        table[name + "b"] = ((planes, rows, width), F32)
     for index in range(3):
         rows, wide = shape.rows[index], shape.wide[index]
         if shape.inside:
@@ -407,7 +410,6 @@
 
     def put_stats(key, rows, first, second=None):
         slot = own_slot(key)
-        slot[...] = jnp.zeros(slot.shape, F32)
         for group in range(2):
             a = b = None
             for g, rng in seg_rows(rows):
@@ -557,9 +559,23 @@
 
     links.put(rows_half(other), r_("wback"), partner, back_slot)
     put_stats("s1", 2, *squares(pre1))
+    slot_ref = own_slot("s1")
+    slot_ref[4:8, :] = jnp.zeros((4, HALF), F32)
+    lane = lax.broadcasted_iota(jnp.int32, (1, LINE), 1)
+    tally = jnp.zeros((1, LINE), F32)
+    for number, name in enumerate(("labels", "depth_valid", "normal_valid")):
+        for group, size in enumerate(("small_", "large_")):
+            value = r_(size + name)[...]
+            keep = (value >= 0).astype(F32) if number == 0 else value.astype(F32)
+            count = jnp.sum(keep, axis=1, keepdims=True)
+            tally = tally + jnp.where(lane == 2 * number + group, count, 0.0)
+    slot_ref[4:5, 0:LINE] = tally
     gather_on(1)
     gather_on(2)
-    mean1, inv1 = moments(add_up("s1"))
+    sums = add_up("s1")
+    mean1, inv1 = moments(sums)
+    tallies = r_("tallies")
+    tallies[...] = sums[4:8, 0:LINE]
     gain, bias = norm1
     for group, rng in seg_rows(2):
         hat = (pre1[rng, :] - mean1[group]) * inv1[group]
@@ -733,19 +749,11 @@
     labels, depth, normals = marks[0:1, :], values[0:1, :], values[8:11, :]
     seg_keep = (labels >= 0).astype(F32)
     depth_keep, normal_keep = marks[1:2, :].astype(F32), marks[2:3, :].astype(F32)
-    lane = lax.broadcasted_iota(jnp.int32, (1, LINE), 1)
     small_lane = lane < WS
     put_stats("sh", 1, *squares(preh))
-    slot_ref = own_slot("sh")
-    tally = jnp.zeros((1, LINE), F32)
-    for number, keep in enumerate((seg_keep, depth_keep, normal_keep)):
-        for group in range(2):
-            count = jnp.sum(jnp.where(small_lane == (group == 0), keep, 0.0), axis=1, keepdims=True)
-            tally = tally + jnp.where(lane == 2 * number + group, count, 0.0)
-    slot_ref[4:5, 0:LINE] = tally
     sums = add_up("sh")
     meanh, invh = moments(sums)
-    tally = sums[4:5, 0:LINE]
+    tally = tallies[0:1, :]
 
     def pixel_count(number):
         picked = [jnp.sum(jnp.where(lane == 2 * number + group, tally, 0.0), axis=1, keepdims=True) for group in range(2)]
@@ -817,8 +825,7 @@
         links.landed(dpx.at[index // 2, index % 2], slot + index)
     links.put(dpx.at[near_block], dpx.at[near_border], partner, slot + 2 * near_border)
     links.put(dpx.at[far_block], dpx.at[far_border], far_chip, slot + 2 * far_border, has_far)
-    links.landed(dpx.at[0], slot, has_low)
-    links.landed(dpx.at[5], slot + 10, has_high)
+    border_slot = slot
 
     dks, dkr, dku, dkg = r_("dks"), r_("dkr"), r_("dku"), r_("dkg")
 
@@ -841,6 +848,48 @@
     lax.fori_loop(0, TAPS, their_tap, 0)
     swap_slot = links.slots()
     links.put(dks, dkr, partner, swap_slot)
+    def my_tap(tap, carry):
+        dku[tap] = tap_grad(tap, s).astype(BF16)
+        return carry
+
+    lax.fori_loop(0, TAPS, my_tap, 0)
+    links.landed(dkr, swap_slot)
+
+    def both(tap, carry):
+        dku[tap] = (dku[tap].astype(F32) + dkr[tap].astype(F32)).astype(BF16)
+        return carry
+
+    lax.fori_loop(0, TAPS, both, 0)
+
+    grad_slot = links.slots(teams * TAPS)
+    grad_out = links.outs(TAPS * halves)
+
+    def grad_copy(number):
+        tap, place = number // halves, number % halves
+        chunk = rank * share + s * halves + place
+        overall = tap * dp + chunk
+        owner, index = overall // TAPS, overall % TAPS
+        src = dku.at[tap, pl.ds(pl.multiple_of(place * unit, unit), unit)]
+        dst = dkg.at[team, index]
+        at = grad_slot + team * TAPS + index
+        to_core = jnp.where(owner == d, other, s)
+        remote = lambda: links.copy(src, dst, (to_core, owner), grad_out + number, at)
+        local = lambda: pltpu.make_async_copy(src, dst, links.recv.at[at])
+        return owner == d, remote, local
+
+    def grad_start(number):
+        mine, remote, local = grad_copy(number)
+        pl.when(mine)(lambda: local().start())
+        pl.when(jnp.logical_not(mine))(lambda: remote().start())
+
+    def grad_done(number):
+        mine, remote, _ = grad_copy(number)
+        pl.when(jnp.logical_not(mine))(lambda: remote().wait_send())
+
+    lax.fori_loop(0, TAPS * halves, lambda i, c: (grad_start(i), c)[1], 0)
+    links.open.append(lambda: lax.fori_loop(0, TAPS * halves, lambda i, c: (grad_done(i), c)[1], 0))
+    links.landed(dpx.at[0], border_slot, has_low)
+    links.landed(dpx.at[5], border_slot + 10, has_high)
 
     dps, grads = r_("dps"), r_("grads")
     for task in range(3):
@@ -878,64 +927,22 @@
         for group, rng in seg_rows(2):
             block = [grads[task, index, rng, :] for task in range(3)]
             for number, (i, j) in enumerate(pairs):
-                sums[6 * group + number] += jnp.sum(block[i] * block[j], axis=0, keepdims=True)
+                sums[len(pairs) * group + number] += jnp.sum(block[i] * block[j], axis=0, keepdims=True)
         return tuple(sums)
 
     sums = lax.fori_loop(0, 4, dots, (jnp.zeros((1, CH), F32),) * (2 * len(pairs)))
-    slot_ref = own_slot("gm")
-    slot_ref[0:16, :] = jnp.zeros((16, HEADW), F32)
+    tally = jnp.zeros((8, LINE), F32)
     for number, total_row in enumerate(sums):
-        slot_ref[number:number + 1, :] = total_row
-    slot_ref[16:, :] = d_proj[...]
+        tally = tally + jnp.where(lane == number, jnp.sum(total_row, axis=1, keepdims=True), 0.0)
+    own_slot("gm")[...] = tally
     near_done = plane_sum("gm", None)
 
-    def my_tap(tap, carry):
-        dku[tap] = tap_grad(tap, s).astype(BF16)
-        return carry
-
-    lax.fori_loop(0, TAPS, my_tap, 0)
-    links.landed(dkr, swap_slot)
-
-    def both(tap, carry):
-        dku[tap] = (dku[tap].astype(F32) + dkr[tap].astype(F32)).astype(BF16)
-        return carry
-
-    lax.fori_loop(0, TAPS, both, 0)
-
-    grad_slot = links.slots(teams * TAPS)
-    grad_out = links.outs(TAPS * halves)
-
-    def grad_copy(number):
-        tap, place = number // halves, number % halves
-        chunk = rank * share + s * halves + place
-        overall = tap * dp + chunk
-        owner, index = overall // TAPS, overall % TAPS
-        src = dku.at[tap, pl.ds(pl.multiple_of(place * unit, unit), unit)]
-        dst = dkg.at[team, index]
-        at = grad_slot + team * TAPS + index
-        to_core = jnp.where(owner == d, other, s)
-        remote = lambda: links.copy(src, dst, (to_core, owner), grad_out + number, at)
-        local = lambda: pltpu.make_async_copy(src, dst, links.recv.at[at])
-        return owner == d, remote, local
-
-    def grad_start(number):
-        mine, remote, local = grad_copy(number)
-        pl.when(mine)(lambda: local().start())
-        pl.when(jnp.logical_not(mine))(lambda: remote().start())
-
-    def grad_done(number):
-        mine, remote, _ = grad_copy(number)
-        pl.when(jnp.logical_not(mine))(lambda: remote().wait_send())
-
-    lax.fori_loop(0, TAPS * halves, lambda i, c: (grad_start(i), c)[1], 0)
-    links.open.append(lambda: lax.fori_loop(0, TAPS * halves, lambda i, c: (grad_done(i), c)[1], 0))
 
     far_done = line_sum("gm", near_done())
-    gram_rows = far_done()
-    r_("proj_o")[...] = gram_rows[16:, :]
-    dot_of = jnp.sum(gram_rows[0:16, :], axis=1, keepdims=True)
+    gram_row = far_done()[0:1, :]
+    dot_of = [jnp.sum(jnp.where(lane == k, gram_row, 0.0), axis=1, keepdims=True) for k in range(2 * len(pairs))]
     gram = {
-        pair: jnp.where(lane == 0, dot_of[k:k + 1, :], dot_of[6 + k:7 + k, :]) for k, pair in enumerate(pairs)
+        pair: jnp.where(lane == 0, dot_of[k], dot_of[len(pairs) + k]) for k, pair in enumerate(pairs)
     }
     alphas = jacobi_weights(gram)
     alphas = [[alpha[:, group:group + 1] for alpha in alphas] for group in range(2)]
@@ -950,6 +957,9 @@
         links.put_or_keep(
             doutb.at[index], dout.at[rank % 4], (seat, chip), slot + rank % 4, (seat == s) & (rank % 4 == index)
         )
+
+    own_slot("pj")[...] = d_proj[...]
+    proj_near = plane_sum("pj", None)
 
     for index in range(4):
         links.landed(dout.at[index], slot + index)
@@ -1055,7 +1065,6 @@
         value = half2[s, rng, :] + half2r[rng, :]
         dy2[rng, :] = value * slope(pre2[rng, :] * gain + bias)
     put_stats("t2", 2, *with_hat(dy2, pre2))
-    advance(third)
     sums = add_up("t2")
     vec[s, 2:3, 0:HALF] = sums[1:2, :] + sums[3:4, :]
     vec[s, 2:3, HALF:2 * HALF] = sums[0:1, :] + sums[2:3, :]
@@ -1064,6 +1073,7 @@
     slot = links.slots(2)
     links.put(dp2.at[1], dp2.at[2], (s, above), slot, has_above)
     links.put(dp2.at[1], dp2.at[0], (s, below), slot + 1, has_below)
+    advance(third)
 
     @pl.when(jnp.logical_not(has_above))
     def _():
@@ -1078,7 +1088,6 @@
             at = tap * BOT + half * HALF
             put_rows(grad_of(1), at, mm(act1s[tap % 3, tap // 3, half], dp2[1], TN).astype(BF16))
     second = reduced(1)
-    advance(third)
     links.landed(dp2.at[2], slot, has_below)
     links.landed(dp2.at[0], slot + 1, has_above)
     acc = None
@@ -1094,7 +1103,7 @@
     half1[0], half1[1] = acc[:, :HALF], acc[:, HALF:]
     slot = links.slots()
     links.put(half1.at[other], half1r, partner, slot)
-    advance(second)
+    advance(third)
     links.landed(half1r, slot)
     dy1, dp1 = r_("dy1"), r_("dp1")
     gain, bias = norm1
@@ -1117,18 +1126,6 @@
         put_rows(grad_of(0), part_index * BOT, mm(x[:, cols], dp1[s], TN).astype(BF16))
     first = reduced(0)
     advance(second)
-    advance(third)
-
-    links.landed(r_("wback"), back_slot)
-    links.landed(dp1.at[other], slot)
-    value = mm(dp1[s], rows_half(s)[...].reshape(WIDE, HALF), NT)
-    value = value + mm(dp1[other], r_("wback")[...].reshape(WIDE, HALF), NT) + du[...]
-    for line in range(2):
-        r_("small_grad_o")[line * WS:(line + 1) * WS, :] = value[line * LINE:line * LINE + WS, :]
-        r_("large_grad_o")[line * WL:(line + 1) * WL, :] = value[line * LINE + WS:(line + 1) * LINE, :]
-    advance(first)
-    advance(second)
-    advance(first)
 
     result = r_("dk_o")
     done_slot, done_out = links.slots(TAPS), links.outs(TAPS)
@@ -1148,7 +1145,22 @@
 
         return mine, final
 
+    proj_done = line_sum("pj", proj_near())
+
+    links.landed(r_("wback"), back_slot)
+    links.landed(dp1.at[other], slot)
+    value = mm(dp1[s], rows_half(s)[...].reshape(WIDE, HALF), NT)
+    value = value + mm(dp1[other], r_("wback")[...].reshape(WIDE, HALF), NT) + du[...]
+    for line in range(2):
+        r_("small_grad_o")[line * WS:(line + 1) * WS, :] = value[line * LINE:line * LINE + WS, :]
+        r_("large_grad_o")[line * WL:(line + 1) * WL, :] = value[line * LINE + WS:(line + 1) * LINE, :]
+    advance(third)
+    advance(first)
+    advance(second)
+    advance(first)
+    advance(third)
     lax.fori_loop(0, TAPS, lambda i, c: (finish_unit(i), c)[1], 0)
+    advance(second)
 
     def finished(index):
         mine, _, _, _ = unit_at(index)
@@ -1157,10 +1169,10 @@
         pl.when(jnp.logical_not(mine))(lambda: links.landed(result.at[index], done_slot + index))
 
     advance(first)
+    advance(second)
     advance(first)
-    advance(second)
-    advance(third)
     lax.fori_loop(0, TAPS, lambda i, c: (finished(i), c)[1], 0)
+    r_("proj_o")[...] = proj_done()
     links.landed(vec.at[other], vec_slot)
     for index, out_part in enumerate(out_parts):
         links.landed(out_part, out_slot + index)
@@ -1250,7 +1262,7 @@
         "large_grad_o": ((2 * WL, WIDE), F32),
         "dk_o": ((TAPS, shape.unit, HEADS), BF16),
         "vec_o": ((2, 8, WIDE), F32),
-        "head_vec_o": ((8, HEADS), F32),
+        "head_vec_o": ((4, HEADS), F32),
         "proj_o": ((PROJ, HEADW), F32),
     }
     for index in range(3):

time: 352 us -> 336 us (0.955)
  Pallas kernels: 351 us -> 335 us
    pallas_call x1, Pallas kernels: 346 us -> 330 us  [call(): pl.pallas_call(functools.partial(fused, shape, names, used), out_shape=[j...]
where the time goes in v2:
time: 336 us
  Pallas kernels  335 us (100%)
    pallas_call x1, Pallas kernels, call(): pl.pallas_call(functools.partial(fused, shape, names, used), out_shape=[j...  330 us

profile of v2, /device:TPU:1, one launch (start us, length us, event | category | flops | bytes accessed | tf_op | source)
XLA Modules:
  0.0 336.0 jit_solution(11323640924742684639)
XLA Ops:
  0.7 330.0 %fused.1 = (bf16[96,2048]{1,0:T(8,128)(2,1)}, bf16[160,2048]{1,0:T(8,128)(2,1)}, f32[96,1024]{1,0:T(8,128)}, f32[160,1024]{1,0:T(8,128)}, bf16[9,128,768]{2,1,0:...) custom-call(bf16[128,512]{1,0:T(8,128)(2,1)} %refs_0_.1, ...), custom_call_target="tpu_custom_call" | custom-call | tf_op jit(solution)/shard_map/fused/pallas_call | solution.py:1279
  330.6 5.2 %finish.1 = (bf16[96,2048]{1,0:T(8,128)(2,1)}, bf16[160,2048]{1,0:T(8,128)(2,1)}, f32[96,1024]{1,0:T(8,128)}, f32[160,1024]{1,0:T(8,128)}, f32[128,512]{1,0:T(8,...) custom-call(bf16[96,2048]{1,0:T(8,128)(2,1)} %get-tuple-element.49.r, ...), custom_call_target="tpu_custom_call" | custom-call | tf_op jit(solution)/shard_map/finish/pallas_call | solution.py:1321

commit v3 on v2

--- a/solution.py
+++ b/solution.py
@@ -841,26 +841,18 @@
             acc = term if acc is None else acc + term
         return acc
 
+    swap_slot, swap_out = links.slots(TAPS), links.outs(TAPS)
+
+    def swap(tap):
+        return links.copy(dks.at[tap], dkr.at[tap], partner, swap_out + tap, swap_slot + tap)
+
     def their_tap(tap, carry):
         dks[tap] = tap_grad(tap, other).astype(BF16)
+        swap(tap).start()
         return carry
 
     lax.fori_loop(0, TAPS, their_tap, 0)
-    swap_slot = links.slots()
-    links.put(dks, dkr, partner, swap_slot)
-    def my_tap(tap, carry):
-        dku[tap] = tap_grad(tap, s).astype(BF16)
-        return carry
-
-    lax.fori_loop(0, TAPS, my_tap, 0)
-    links.landed(dkr, swap_slot)
-
-    def both(tap, carry):
-        dku[tap] = (dku[tap].astype(F32) + dkr[tap].astype(F32)).astype(BF16)
-        return carry
-
-    lax.fori_loop(0, TAPS, both, 0)
-
+    links.open.append(lambda: lax.fori_loop(0, TAPS, lambda i, c: (swap(i).wait_send(), c)[1], 0))
     grad_slot = links.slots(teams * TAPS)
     grad_out = links.outs(TAPS * halves)
 
@@ -886,7 +878,14 @@
         mine, remote, _ = grad_copy(number)
         pl.when(jnp.logical_not(mine))(lambda: remote().wait_send())
 
-    lax.fori_loop(0, TAPS * halves, lambda i, c: (grad_start(i), c)[1], 0)
+    def my_tap(tap, carry):
+        value = tap_grad(tap, s)
+        links.landed(dkr.at[tap], swap_slot + tap)
+        dku[tap] = (value + dkr[tap].astype(F32)).astype(BF16)
+        several(halves, lambda place: grad_start(tap * halves + place))
+        return carry
+
+    lax.fori_loop(0, TAPS, my_tap, 0)
     links.open.append(lambda: lax.fori_loop(0, TAPS * halves, lambda i, c: (grad_done(i), c)[1], 0))
     links.landed(dpx.at[0], border_slot, has_low)
     links.landed(dpx.at[5], border_slot + 10, has_high)

time: 336 us -> 342 us (1.018)
  Pallas kernels: 335 us -> 341 us
    pallas_call x1, Pallas kernels: 330 us -> 335 us  [call(): pl.pallas_call(functools.partial(fused, shape, names, used), out_shape=[j...]
where the time goes in v3:
time: 342 us
  Pallas kernels  341 us (100%)
    pallas_call x1, Pallas kernels, call(): pl.pallas_call(functools.partial(fused, shape, names, used), out_shape=[j...  335 us

profile of v3, /device:TPU:1, one launch (start us, length us, event | category | flops | bytes accessed | tf_op | source)
XLA Modules:
  0.0 341.5 jit_solution(1436847554241330153)
XLA Ops:
  0.7 335.4 %fused.1 = (bf16[96,2048]{1,0:T(8,128)(2,1)}, bf16[160,2048]{1,0:T(8,128)(2,1)}, f32[96,1024]{1,0:T(8,128)}, f32[160,1024]{1,0:T(8,128)}, bf16[9,128,768]{2,1,0:...) custom-call(bf16[128,512]{1,0:T(8,128)(2,1)} %refs_0_.1, ...), custom_call_target="tpu_custom_call" | custom-call | tf_op jit(solution)/shard_map/fused/pallas_call | solution.py:1278
  336.1 5.2 %finish.1 = (bf16[96,2048]{1,0:T(8,128)(2,1)}, bf16[160,2048]{1,0:T(8,128)(2,1)}, f32[96,1024]{1,0:T(8,128)}, f32[160,1024]{1,0:T(8,128)}, f32[128,512]{1,0:T(8,...) custom-call(bf16[96,2048]{1,0:T(8,128)(2,1)} %get-tuple-element.49.r, ...), custom_call_target="tpu_custom_call" | custom-call | tf_op jit(solution)/shard_map/finish/pallas_call | solution.py:1320
